TPU v7x, 32 devices: a whole 2x2x4 slice. The times are simulated.
32 devices in a mesh: seq: 8 (over z, x), head: 4 (over y, core).
Axes of the slice: x: 2, y: 2, z: 4, core: 2. Of those that a mesh axis runs over, the one named last changes fastest.
Arguments:
- queries: bfloat16 [8192, 5120], P('seq', 'head')
- keys: bfloat16 [8192, 5120], P('seq', 'head')
- values: bfloat16 [8192, 5120], P('seq', 'head'), may hold values from -6 to 6
- query_gain: float32 [5120], P('head'), may hold values from 0.1 to 1.9
- key_gain: float32 [5120], P('head'), may hold values from 0.1 to 1.9
- shapes: int32 [2, 3], replicated, may hold values from 4 to 32, as said below
- windows: int32 [64, 27], P('seq'), may hold values from -1 to 63, as said below
- text_keys: bfloat16 [8, 256, 5120], P(None, 'seq', 'head')
- text_values: bfloat16 [8, 256, 5120], P(None, 'seq', 'head'), may hold values from -6 to 6
- owner: int32 [2], replicated, may hold values from 0 to 7, as said below
Outputs:
- attended: bfloat16 [8192, 5120], P('seq', 'head')
Inputs may be any that keep to these rules, and one draw needn't show every extreme that they name: `shapes`: row s is (frames, height, width) of video s in tokens: height and width are 16 and 32, or 32 and 16, so a frame has 4 tiles; each video has from 16 to 48 tiles, and the videos' tiles add up to 64, so no tile holds tokens of two videos. `windows`: entry k of row g stands for the tile k // 9 - 1 frames, (k // 3) % 3 - 1 tile rows and k % 3 - 1 tile columns away from tile g in its video: it holds that tile's number or -1; it is -1 wherever that tile lies outside the video, and entry 13 is always g. `owner`: no two videos share a panel.
All inputs are finite; a program needn't handle non-finite values.
Results may differ from a plain program's by a relative error of at most 0.012.
Values may be sent and summed in bfloat16 or wider, within the bound.
No kernel may reach another device: no remote copies, remote signals or barrier semaphores. Data moves between devices by JAX's collectives and lax.ppermute only.
A program may use at most 192 MiB of HBM per device.

v0:
```python
import jax
import jax.numpy as jnp
from jax import lax
from jax.sharding import PartitionSpec as P

HEAD_DIM = 128
D = 5120
TILE_H = 8
TILE_W = 16
REACH = 7
TXT = 256


epsilon = 1e-06


def extended_2(cells, sides, width):
    for axis, dim in sides:
        count = lax.axis_size(axis)
        ends = count - 1
        head = lax.slice_in_dim(cells, 0, width, axis=dim)
        tail = lax.slice_in_dim(cells, cells.shape[dim] - width, cells.shape[dim], axis=dim)
        cells = jnp.concatenate(
            [
                lax.ppermute(tail, axis, [(i, (i + 1) % count) for i in range(ends)]),
                cells,
                lax.ppermute(head, axis, [((i + 1) % count, i) for i in range(ends)]),
            ],
            axis=dim,
        )
    return cells


def tile_table(shape_rows):
    per_frame = shape_rows[:, 1] // TILE_H * (shape_rows[:, 2] // TILE_W)
    tile_counts = shape_rows[:, 0] * per_frame
    tile_ends = jnp.cumsum(tile_counts)
    return (tile_ends - tile_counts, tile_ends)


def locate(tile_ids, shape_rows, tile_starts, tile_ends):
    sample_ids = jnp.sum((tile_ids[:, None] >= tile_ends[None, :]).astype(jnp.int32), axis=1)
    one_hot = (
        sample_ids[:, None] == jnp.arange(tile_ends.shape[0], dtype=jnp.int32)[None, :]
    ).astype(jnp.int32)
    first_tiles = jnp.sum(one_hot * tile_starts[None, :], axis=1)
    row_counts = jnp.sum(one_hot * (shape_rows[:, 1] // TILE_H)[None, :], axis=1)
    col_counts = jnp.sum(one_hot * (shape_rows[:, 2] // TILE_W)[None, :], axis=1)
    offsets = tile_ids - first_tiles
    per_frame = row_counts * col_counts
    within = offsets % per_frame
    return (sample_ids, one_hot, offsets // per_frame, within // col_counts, within % col_counts)


def rope_angles(frames, bands, columns, head_size):
    inner = jnp.arange(TILE_H * TILE_W, dtype=jnp.int32)
    tile_total = frames.shape[0]
    time_pos = (
        jnp.broadcast_to(frames[:, None], (tile_total, inner.shape[0]))
        .reshape(-1)
        .astype(jnp.float32)
    )
    row_pos = (bands[:, None] * TILE_H + inner[None, :] // TILE_W).reshape(-1).astype(jnp.float32)
    col_pos = (columns[:, None] * TILE_W + inner[None, :] % TILE_W).reshape(-1).astype(jnp.float32)
    third = head_size // 6
    part_sizes = (head_size - 4 * third, 2 * third, 2 * third)
    angle_parts = []
    for position, part_size in zip((time_pos, row_pos, col_pos), part_sizes):
        frequency = 10000.0 ** (-jnp.arange(0, part_size, 2, dtype=jnp.float32) / part_size)
        angle_parts.append(position[:, None] * frequency[None, :])
    return jnp.concatenate(angle_parts, axis=1)


def rotate(field, angles):
    paired = field.reshape(field.shape[0], field.shape[1], field.shape[2] // 2, 2)
    cosine = jnp.cos(angles)[:, None, :]
    sine = jnp.sin(angles)[:, None, :]
    even_part = paired[..., 0]
    odd_part = paired[..., 1]
    turned = jnp.stack(
        [even_part * cosine - odd_part * sine, even_part * sine + odd_part * cosine], axis=-1
    )
    return turned.reshape(field.shape)


def finish_rows(widened, squares, gain, angles, head_count):
    scaled = widened * lax.rsqrt(squares / D + epsilon)[:, None] * gain[None, :]
    turned = rotate(scaled.reshape(widened.shape[0], head_count, HEAD_DIM), angles)
    return turned.reshape(widened.shape).astype(jnp.bfloat16)


def local(
    queries, keys, values, query_gain, key_gain, shapes, windows, text_keys, text_values, owner
):
    row_count, feat_width = queries.shape
    head_count = feat_width // HEAD_DIM
    tile_rows = TILE_H * TILE_W
    tiles_here = row_count // tile_rows
    first_global = lax.axis_index("seq") * tiles_here
    tile_starts, tile_ends = tile_table(shapes)
    tile_ids = first_global + jnp.arange(tiles_here, dtype=jnp.int32)
    sample_ids, one_hot, frames, bands, columns = locate(tile_ids, shapes, tile_starts, tile_ends)
    angles = rope_angles(frames, bands, columns, HEAD_DIM)
    query_wide = queries.astype(jnp.float32)
    key_wide = keys.astype(jnp.float32)
    query_squares, key_squares = lax.psum(
        (jnp.sum(query_wide * query_wide, axis=1), jnp.sum(key_wide * key_wide, axis=1)), "head"
    )
    q_hat = finish_rows(query_wide, query_squares, query_gain, angles, head_count)
    k_hat = finish_rows(key_wide, key_squares, key_gain, angles, head_count)
    key_value = jnp.stack([k_hat, values])
    extended = extended_2(key_value, (("seq", 1),), REACH * tile_rows)
    panel_of_tile = jnp.sum(one_hot * owner[None, :], axis=1)
    prompt_pair = jnp.stack([text_keys, text_values])
    every_panel = lax.all_gather(prompt_pair, "seq", axis=2, tiled=True)
    wanted = jnp.stack([panel_of_tile[0], panel_of_tile[tiles_here - 1]])
    panels = jnp.take(every_panel, wanted, axis=1)
    prompt_keys = panels[0].reshape(2 * TXT, head_count, HEAD_DIM)
    prompt_values = panels[1].reshape(2 * TXT, head_count, HEAD_DIM)
    second_slot = (sample_ids != sample_ids[0]).astype(jnp.int32)
    prompt_allowed = second_slot[:, None] == (jnp.arange(2 * TXT, dtype=jnp.int32) // TXT)[None, :]
    key_tiles = first_global - REACH + jnp.arange(tiles_here + 2 * REACH, dtype=jnp.int32)
    window_allowed = (
        jnp.any(windows[:, :, None] == key_tiles[None, None, :], axis=1) & (key_tiles >= 0)[None, :]
    )
    group_tiles = 4
    span_tiles = group_tiles + 2 * REACH
    group_rows = group_tiles * tile_rows
    factor = HEAD_DIM ** (-0.5)

    def attend(block_index):
        start_tile = block_index * group_tiles
        query_rows = lax.dynamic_slice_in_dim(q_hat, start_tile * tile_rows, group_rows, 0).reshape(
            group_rows, head_count, HEAD_DIM
        )
        key_rows = lax.dynamic_slice_in_dim(
            extended[0], start_tile * tile_rows, span_tiles * tile_rows, 0
        ).reshape(span_tiles * tile_rows, head_count, HEAD_DIM)
        value_rows = lax.dynamic_slice_in_dim(
            extended[1], start_tile * tile_rows, span_tiles * tile_rows, 0
        ).reshape(span_tiles * tile_rows, head_count, HEAD_DIM)
        allowed = lax.dynamic_slice(
            window_allowed, (start_tile, start_tile), (group_tiles, span_tiles)
        )
        prompt_ok = lax.dynamic_slice_in_dim(prompt_allowed, start_tile, group_tiles, 0)
        key_mask = jnp.concatenate(
            [
                jnp.repeat(jnp.repeat(allowed, tile_rows, axis=0), tile_rows, axis=1),
                jnp.repeat(prompt_ok, tile_rows, axis=0),
            ],
            axis=1,
        )
        all_keys = jnp.concatenate([key_rows, prompt_keys], axis=0)
        all_values = jnp.concatenate([value_rows, prompt_values], axis=0)
        scores = (
            jnp.einsum("qhd,khd->hqk", query_rows, all_keys, preferred_element_type=jnp.float32)
            * factor
        )
        scores = jnp.where(key_mask[None, :, :], scores, -jnp.inf)
        largest = jnp.max(scores, axis=-1, keepdims=True)
        weights = jnp.exp(scores - largest)
        totals = jnp.sum(weights, axis=-1)
        mixed = jnp.einsum(
            "hqk,khd->qhd",
            weights.astype(jnp.bfloat16),
            all_values,
            preferred_element_type=jnp.float32,
        )
        mixed = mixed / jnp.transpose(totals)[:, :, None]
        return mixed.astype(jnp.bfloat16).reshape(group_rows, feat_width)

    outputs = lax.map(attend, jnp.arange(tiles_here // group_tiles, dtype=jnp.int32))
    return outputs.reshape(row_count, feat_width)


def solution(mesh):
    placed = (
        P("seq", "head"),
        P("seq", "head"),
        P("seq", "head"),
        P("head"),
        P("head"),
        P(),
        P("seq", None),
        P(None, "seq", "head"),
        P(None, "seq", "head"),
        P(),
    )
    return jax.shard_map(
        local, mesh=mesh, in_specs=placed, out_specs=P("seq", "head"), check_vma=False
    )
```

profile of v0, /device:TPU:8, one launch (start us, length us, event | category | flops | bytes accessed | tf_op | source)
XLA Modules:
  0.0 574.4 jit_solution(4502013482315516122)
XLA Ops:
  6.5 2.6 pad_maximum_fusion.4
  10.9 2.3 fusion.24
  13.3 7.1 %all-reduce = (f32[1024]{0:T(1024)S(1)}, f32[1024]{0:T(1024)S(1)}) all-reduce(f32[1024]{0:T(1024)S(1)} %fusion.22, f32[1024]{0:T(1024)S(1)} %fusion.24), channel_id=1, replica_groups=mesh['seq'=8,'head'=4] {'head'}, use_global_device_ids=true, to_apply=%region_8.9 | all-reduce | flops 2048 | bytes 16384 | tf_op jit(solution)/shard_map/psum | solution.py:106
  20.4 3.0 fusion.23
  23.3 6.0 %copy.28 = f32[1024,1280]{0,1:T(8,128)} copy(f32[1024,1280]{1,0:T(8,128)} %fusion.23) | data formatting | bytes 10485760 | tf_op jit(solution)/shard_map/mul | solution.py:87
  29.3 7.7 %reshape_reshape.8 = f32[1024,10,64,2]{0,3,2,1:T(2,128)} reshape(f32[1024,1280]{0,1:T(8,128)} %copy.28) | data formatting | bytes 10485760 | tf_op jit(solution)/shard_map/reshape;reshape | solution.py:75
  37.0 2.8 fusion.25
  39.8 6.0 %copy.31 = f32[1024,1280]{0,1:T(8,128)} copy(f32[1024,1280]{1,0:T(8,128)} %fusion.25) | data formatting | bytes 10485760 | tf_op jit(solution)/shard_map/mul | solution.py:87
  45.8 7.6 %reshape_reshape.9 = f32[1024,10,64,2]{0,3,2,1:T(2,128)} reshape(f32[1024,1280]{0,1:T(8,128)} %copy.31) | data formatting | bytes 10485760 | tf_op jit(solution)/shard_map/reshape;reshape | solution.py:75
  55.3 16.5 %subtract_convert_fusion = (bf16[1024,10,64,1]{0,3,2,1:T(2,128)(2,1)}, bf16[1024,10,64,1]{0,3,2,1:T(2,128)(2,1)}, bf16[1024,10,64,1]{0,3,2,1:T(2,128)(2,1)S(1)}, bf16[1024,10,64,1]{0,3,2,1:T(2,128)(2,1)S(1)}) fusion(f32[1024,10,64,2]{0,3,2,1:T(2,128)} %reshape_reshape.9, f32[1024,64]{0,1:T(8,128)S(1)} %get-tuple-element.186, ...), kind=kLoop, calls=%fused_computation.46 | loop fusion | flops 10485760 | bytes 16252928 | tf_op jit(solution)/shard_map/convert.2
  71.8 6.8 %pad_maximum_fusion.2 = bf16[1024,10,64,2]{0,3,2,1:T(2,128)(2,1)} fusion(bf16[1024,10,64,1]{0,3,2,1:T(2,128)(2,1)S(1)} %get-tuple-element.183, bf16[1024,10,64,1]{0,3,2,1:T(2,128)(2,1)S(1)} %get-tuple-element.184), kind=kLoop, calls=%fused_computation.42 | loop fusion | flops 5242880 | bytes 5242880 | tf_op jit(solution)/shard_map/stack | solution.py:80
  78.6 3.8 convert_element_type.83
  82.4 4.5 copy.29
  86.9 6.2 %fusion.26 = (bf16[2,896,1280]{1,2,0:T(8,128)(2,1)}, bf16[2,896,1280]{1,2,0:T(8,128)(2,1)}) fusion(bf16[1,1024,1280]{1,2,0:T(8,128)(2,1)S(1)} %convert_element_type.83, bf16[1,1024,1280]{1,2,0:T(8,128)(2,1)} %bitcast.92), kind=kLoop, calls=%fused_computation.40 | loop fusion | flops 18350080 | bytes 14417920 | tf_op jit(solution)/shard_map/stack | solution.py:111
  93.1 3.4 collective-permute-start
  96.5 3.5 collective-permute-start.1
  100.0 8.1 %pad_maximum_fusion.3 = bf16[1024,10,64,2]{0,3,2,1:T(2,128)(2,1)} fusion(bf16[1024,10,64,1]{0,3,2,1:T(2,128)(2,1)} %get-tuple-element.176, bf16[1024,10,64,1]{0,3,2,1:T(2,128)(2,1)} %get-tuple-element.175), kind=kLoop, calls=%fused_computation.43 | loop fusion | flops 5242880 | bytes 5242880 | tf_op jit(solution)/shard_map/stack | solution.py:80
  108.1 5.2 convert_element_type.86
  113.9 1.3 fusion.33
  115.2 1.3 compare_and_fusion
  117.3 206.8 %collective-permute-done = bf16[2,896,1280]{1,2,0:T(8,128)(2,1)} collective-permute-done((bf16[2,896,1280]{1,2,0:T(8,128)(2,1)}, bf16[2,896,1280]{1,2,0:T(8,128)(2,1)}, u32[]{:S(2)}, u32[]{:S(2)}) %collective-permute-start) | collective-permute-done | bytes 4587552 | tf_op jit(solution)/shard_map/ppermute | solution.py:25
  324.1 1.9 collective-permute-done.1
  326.0 11.8 %pad_maximum_fusion = bf16[2,2816,1280]{1,2,0:T(8,128)(2,1)} fusion(bf16[2,896,1280]{1,2,0:T(8,128)(2,1)} %collective-permute-done.1, bf16[1,1024,1280]{1,2,0:T(8,128)(2,1)} %bitcast.93, bf16[1,1024,1280]{1,2,0:T(8,128)(2,1)S(1)} %convert_element_type.83, bf16[2,896,1280]{1,2,0:T(8,128)(2,1)} %collective-permute-done), kind=kLoop, calls=%fused_computation.29 | loop fusion | flops 57671680 | bytes 28835840 | tf_op jit(solution)/shard_map/concatenate | solution.py:23
  337.8 4.7 gather_fusion
  344.1 2.6 reshape.554
  346.8 1.4 copy.33
  349.3 1.7 reshape_squeeze.6
  351.0 216.5 %while.12 = (s32[]{:T(128)}, bf16[2,512,1280]{2,1,0:T(8,128)(2,1)}, bf16[2,2816,1280]{1,2,0:T(8,128)(2,1)}, s32[2]{0:T(128)S(1)}, bf16[512,10,128]{0,2,1:T(8,128...) while((s32[]{:T(128)}, bf16[2,512,1280]{2,1,0:T(8,128)(2,1)}, ...), condition=%wide.region_14.15_spmd, body=%wide.region_11.14_spmd.sunk | while | flops 7572150272 | bytes 284862528 | solution.py:172
  353.0 1.6 broadcast_in_dim.132
  355.3 2.6 copy.51
  358.6 10.2 %fusion.51 = (bf16[1,2816,1280]{1,2,0:T(8,128)(2,1)}, bf16[1,2816,1280]{1,2,0:T(8,128)(2,1)}) fusion(bf16[2,2816,1280]{1,2,0:T(8,128)(2,1)} %get-tuple-element.302), kind=kLoop, calls=%fused_computation.124.clone.1 | loop fusion | bytes 28835840 | tf_op jit(solution)/shard_map/while/body/eval_jaxpr/slice | solution.py:140
  368.8 9.5 %constant_dynamic-slice_fusion.9 = (bf16[1,2304,1280]{1,2,0:T(8,128)(2,1)}, bf16[1,2304,1280]{1,2,0:T(8,128)(2,1)}) fusion(bf16[1,2816,1280]{1,2,0:T(8,128)(2,1)} %get-tuple-element.258, s32[]{:T(128)S(6)} %select_n.247, bf16[1,2816,1280]{1,2,0:T(8,128)(2,1)} %get-tuple-element.259), kind=kLoop, calls=%fused_computation.21.clone.1 | loop fusion | bytes 23592964 | tf_op jit(solution)/shard_map/while/body/eval_jaxpr/dynamic_slice | solution.py:136
  378.3 9.0 %copy.52 = bf16[2304,10,128]{2,0,1:T(8,128)(2,1)} copy(bf16[2304,10,128]{0,2,1:T(8,128)(2,1)} %bitcast.85) | data formatting | bytes 11796480 | tf_op jit(solution)/shard_map/while/body/eval_jaxpr/reshape | solution.py:138
  387.3 1.4 constant_dynamic-slice_fusion.8
  388.7 23.7 %fusion.52 = (f32[10,512]{1,0:T(8,128)S(1)}, f32[10,512,2816]{2,1,0:T(8,128)}) fusion(pred[512,2816]{1,0:T(8,128)(4,1)S(1)} %copy.51, bf16[512,10,128]{0,2,1:T(8,128)(2,1)S(1)} %bitcast.89, bf16[512,10,128]{2,0,1:T(8,128)(2,1)S(1)} %copy-done.2, bf16[2304,10,128]{2,0,1:T(8,128)(2,1)} %copy.52), kind=kOutput, calls=%fused_computation.3.clone.1 | convolution fusion | flops 3748654080 | bytes 67653632 | tf_op jit(solution)/shard_map/while/body/eval_jaxpr/qhd,khd->hqk/dot_general | solution.py:156
  412.4 18.9 %fusion.53 = f32[10,512]{1,0:T(8,128)S(1)} fusion(f32[10,512,2816]{2,1,0:T(8,128)} %get-tuple-element.261, f32[10,512]{1,0:T(8,128)S(1)} %get-tuple-element.262, pred[512,2816]{1,0:T(8,128)(4,1)S(1)} %copy.51), kind=kLoop, calls=%fused_computation.4.clone.1 | loop fusion | flops 57666560 | bytes 59154432 | tf_op jit(solution)/shard_map/while/body/eval_jaxpr/reduce_sum | solution.py:162
  431.3 25.2 %fusion.54 = bf16[512,10,128]{0,2,1:T(8,128)(2,1)} fusion(f32[10,512,2816]{2,1,0:T(8,128)} %get-tuple-element.261, f32[10,512]{1,0:T(8,128)S(1)} %get-tuple-element.262, pred[512,2816]{1,0:T(8,128)(4,1)S(1)} %copy.51, bf16[512,10,128]{0,2,1:T(8,128)(2,1)S(1)} %copy-done.3, bf16[2304,10,128]{0,2,1:T(8,128)(2,1)} %bitcast.86, f32[512,10]{0,1:T(8,128)S(1)} %bitcast.96), kind=kOutput, calls=%fused_computation.17.clone.1 | convolution fusion | flops 3764387840 | bytes 67674112 | tf_op jit(solution)/shard_map/while/body/eval_jaxpr/hqk,khd->qhd/dot_general | solution.py:163
  456.5 1.6 copy.53
  461.3 1.6 broadcast_in_dim.132
  463.5 2.6 copy.51
  466.8 10.2 %fusion.51 = (bf16[1,2816,1280]{1,2,0:T(8,128)(2,1)}, bf16[1,2816,1280]{1,2,0:T(8,128)(2,1)}) fusion(bf16[2,2816,1280]{1,2,0:T(8,128)(2,1)} %get-tuple-element.302), kind=kLoop, calls=%fused_computation.124.clone.1 | loop fusion | bytes 28835840 | tf_op jit(solution)/shard_map/while/body/eval_jaxpr/slice | solution.py:140
  477.1 9.5 %constant_dynamic-slice_fusion.9 = (bf16[1,2304,1280]{1,2,0:T(8,128)(2,1)}, bf16[1,2304,1280]{1,2,0:T(8,128)(2,1)}) fusion(bf16[1,2816,1280]{1,2,0:T(8,128)(2,1)} %get-tuple-element.258, s32[]{:T(128)S(6)} %select_n.247, bf16[1,2816,1280]{1,2,0:T(8,128)(2,1)} %get-tuple-element.259), kind=kLoop, calls=%fused_computation.21.clone.1 | loop fusion | bytes 23592964 | tf_op jit(solution)/shard_map/while/body/eval_jaxpr/dynamic_slice | solution.py:136
  486.5 9.0 %copy.52 = bf16[2304,10,128]{2,0,1:T(8,128)(2,1)} copy(bf16[2304,10,128]{0,2,1:T(8,128)(2,1)} %bitcast.85) | data formatting | bytes 11796480 | tf_op jit(solution)/shard_map/while/body/eval_jaxpr/reshape | solution.py:138
  495.5 1.4 constant_dynamic-slice_fusion.8
  496.9 23.7 %fusion.52 = (f32[10,512]{1,0:T(8,128)S(1)}, f32[10,512,2816]{2,1,0:T(8,128)}) fusion(pred[512,2816]{1,0:T(8,128)(4,1)S(1)} %copy.51, bf16[512,10,128]{0,2,1:T(8,128)(2,1)S(1)} %bitcast.89, bf16[512,10,128]{2,0,1:T(8,128)(2,1)S(1)} %copy-done.2, bf16[2304,10,128]{2,0,1:T(8,128)(2,1)} %copy.52), kind=kOutput, calls=%fused_computation.3.clone.1 | convolution fusion | flops 3748654080 | bytes 67653632 | tf_op jit(solution)/shard_map/while/body/eval_jaxpr/qhd,khd->hqk/dot_general | solution.py:156
  520.6 18.9 %fusion.53 = f32[10,512]{1,0:T(8,128)S(1)} fusion(f32[10,512,2816]{2,1,0:T(8,128)} %get-tuple-element.261, f32[10,512]{1,0:T(8,128)S(1)} %get-tuple-element.262, pred[512,2816]{1,0:T(8,128)(4,1)S(1)} %copy.51), kind=kLoop, calls=%fused_computation.4.clone.1 | loop fusion | flops 57666560 | bytes 59154432 | tf_op jit(solution)/shard_map/while/body/eval_jaxpr/reduce_sum | solution.py:162
  539.5 25.2 %fusion.54 = bf16[512,10,128]{0,2,1:T(8,128)(2,1)} fusion(f32[10,512,2816]{2,1,0:T(8,128)} %get-tuple-element.261, f32[10,512]{1,0:T(8,128)S(1)} %get-tuple-element.262, pred[512,2816]{1,0:T(8,128)(4,1)S(1)} %copy.51, bf16[512,10,128]{0,2,1:T(8,128)(2,1)S(1)} %copy-done.3, bf16[2304,10,128]{0,2,1:T(8,128)(2,1)} %bitcast.86, f32[512,10]{0,1:T(8,128)S(1)} %bitcast.96), kind=kOutput, calls=%fused_computation.17.clone.1 | convolution fusion | flops 3764387840 | bytes 67674112 | tf_op jit(solution)/shard_map/while/body/eval_jaxpr/hqk,khd->qhd/dot_general | solution.py:163
  564.8 1.6 copy.53
  (77 shorter events, 13.9 us)
Async XLA Ops:
  6.5 3.8 copy-start
  6.5 331.3 %all-gather.2.cloned.1.call-start = ((), (), s32[]{:S(2)}) async-start(), calls=%async_computation | async-start | bytes 11796480 | tf_op jit(solution)/shard_map/all_gather | solution.py:115
  6.5 13.8 %copy-start.4 = (f32[1280]{0:T(1024)S(1)}, f32[1280]{0:T(1024)}, u32[]{:S(2)}) copy-start(f32[1280]{0:T(1024)} %param.16) | copy-start | bytes 15364
  29.3 7.7 %copy-start.1 = (bf16[1024,1280]{1,0:T(8,128)(2,1)S(1)}, bf16[1024,1280]{1,0:T(8,128)(2,1)}, u32[]{:S(2)}) copy-start(bf16[1024,1280]{1,0:T(8,128)(2,1)} %param.12) | copy-start | bytes 7864324
  29.3 7.7 %copy-start.5 = (f32[1280]{0:T(1024)S(1)}, f32[1280]{0:T(1024)}, u32[]{:S(2)}) copy-start(f32[1280]{0:T(1024)} %param.15) | copy-start | bytes 15364
  45.8 7.7 %copy-start.7 = (s32[2]{0:T(128)S(1)}, s32[2]{0:T(128)}, u32[]{:S(2)}) copy-start(s32[2]{0:T(128)} %param.21) | copy-start | bytes 28
  93.1 231.0 %collective-permute-start = (bf16[2,896,1280]{1,2,0:T(8,128)(2,1)}, bf16[2,896,1280]{1,2,0:T(8,128)(2,1)}, u32[]{:S(2)}, u32[]{:S(2)}) collective-permute-start(bf16[2,896,1280]{1,2,0:T(8,128)(2,1)} %get-tuple-element.179), channel_id=1, source_target_pairs={{0,4},{4,8},{8,12},{12,16},{16,20},{20,24},{24,28},{1,5},{5,9},{9,... | collective-permute-start | bytes 13762568 | tf_op jit(solution)/shard_map/ppermute | solution.py:25
  96.5 229.5 %collective-permute-start.1 = (bf16[2,896,1280]{1,2,0:T(8,128)(2,1)}, bf16[2,896,1280]{1,2,0:T(8,128)(2,1)}, u32[]{:S(2)}, u32[]{:S(2)}) collective-permute-start(bf16[2,896,1280]{1,2,0:T(8,128)(2,1)} %get-tuple-element.180), channel_id=1, source_target_pairs={{4,0},{8,4},{12,8},{16,12},{20,16},{24,20},{28,24},{5,1},{9,5},{13... | collective-permute-start | bytes 13762568 | tf_op jit(solution)/shard_map/ppermute | solution.py:27
  108.1 8.4 %copy-start.6 = (s32[8,27]{1,0:T(8,128)S(1)}, s32[8,27]{1,0:T(8,128)}, u32[]{:S(2)}) copy-start(s32[8,27]{1,0:T(8,128)} %param.18) | copy-start | bytes 2596
  378.3 10.4 %copy-start.2 = (bf16[512,10,128]{2,0,1:T(8,128)(2,1)S(1)}, bf16[512,10,128]{2,0,1:T(8,128)(2,1)}, u32[]{:S(2)}) copy-start(bf16[512,10,128]{2,0,1:T(8,128)(2,1)} %get-tuple-element.308) | copy-start | bytes 3932164 | tf_op jit(solution)/shard_map/while
  412.4 18.9 %copy-start.3 = (bf16[512,10,128]{0,2,1:T(8,128)(2,1)S(1)}, bf16[512,10,128]{0,2,1:T(8,128)(2,1)}, u32[]{:S(2)}) copy-start(bf16[512,10,128]{0,2,1:T(8,128)(2,1)} %get-tuple-element.304) | copy-start | bytes 3932164 | tf_op jit(solution)/shard_map/while
  486.5 10.4 %copy-start.2 = (bf16[512,10,128]{2,0,1:T(8,128)(2,1)S(1)}, bf16[512,10,128]{2,0,1:T(8,128)(2,1)}, u32[]{:S(2)}) copy-start(bf16[512,10,128]{2,0,1:T(8,128)(2,1)} %get-tuple-element.308) | copy-start | bytes 3932164 | tf_op jit(solution)/shard_map/while
  520.6 18.9 %copy-start.3 = (bf16[512,10,128]{0,2,1:T(8,128)(2,1)S(1)}, bf16[512,10,128]{0,2,1:T(8,128)(2,1)}, u32[]{:S(2)}) copy-start(bf16[512,10,128]{0,2,1:T(8,128)(2,1)} %get-tuple-element.304) | copy-start | bytes 3932164 | tf_op jit(solution)/shard_map/while
Sparse Core Ops, SparseCore 0:
  9.6 277.1 all-gather.1
where the time goes:
time: 576 us; the launch traced here: 574 us
  waiting for transfers between devices  209 us (36%)
  local copies, waits for them, and re-layouts  131 us (23%)
  other arithmetic  106 us (18%)
  matrix products  97.8 us (17%)
  between operations  13.6 us (2%)
  blocking collectives  7.08 us (1%)
  starting transfers between devices  6.91 us (1%)
    ppermute x1, waiting for transfers between devices, extended_2(): lax.ppermute(tail, axis, [(i, (i + 1) % count) for i in range(ends)])  207 us
    dot_general x2, matrix products, attend(): jnp.einsum('hqk,khd->qhd', weights.astype(jnp.bfloat16), all_values, pref...  50.4 us
    dot_general x2, matrix products, attend(): jnp.einsum('qhd,khd->hqk', query_rows, all_keys, preferred_element_type=j...  47.4 us
    reduce_sum x2, other arithmetic, attend(): totals = jnp.sum(weights, axis=-1)  37.8 us
    slice x2, local copies, waits for them, and re-layouts, attend(): extended[1]  20.4 us
    dynamic_slice x2, local copies, waits for them, and re-layouts, attend(): lax.dynamic_slice_in_dim(extended[0], start_tile * tile_rows, span_tiles...  19 us
    reshape x2, local copies, waits for them, and re-layouts, attend(): key_rows = lax.dynamic_slice_in_dim(extended[0], start_tile * tile_rows,...  18 us
    another operation x3, other arithmetic  16.6 us
  transfers between devices with their start and end apart: 3, of which 2 were waited for; matrix products, arithmetic and copies ran while one was open for 18% of the time, Pallas kernels for 0%

commit v1 on v0

v1 whole, which is shorter than its diff:
```python
import functools
import math

import jax
import jax.numpy as jnp
import numpy as np
from jax import lax
from jax.experimental import pallas as pl
from jax.experimental.pallas import tpu as pltpu
from jax.sharding import PartitionSpec as P

HEAD_DIM = 128
D = 5120
TILE_H = 8
TILE_W = 16
TILE = 128
FRAME_TILES = 4
FRAME = FRAME_TILES * TILE
TXT = 256
EPSILON = 1e-06
OUT_OF_WINDOW = -1e30


def tile_positions(tile_ids, shapes):
    per_frame = shapes[:, 1] // TILE_H * (shapes[:, 2] // TILE_W)
    tile_counts = shapes[:, 0] * per_frame
    tile_ends = jnp.cumsum(tile_counts)
    tile_starts = tile_ends - tile_counts
    sample_ids = jnp.sum((tile_ids[:, None] >= tile_ends[None, :]).astype(jnp.int32), axis=1)
    one_hot = (
        sample_ids[:, None] == jnp.arange(shapes.shape[0], dtype=jnp.int32)[None, :]
    ).astype(jnp.int32)
    first_tiles = jnp.sum(one_hot * tile_starts[None, :], axis=1)
    row_counts = jnp.sum(one_hot * (shapes[:, 1] // TILE_H)[None, :], axis=1)
    col_counts = jnp.sum(one_hot * (shapes[:, 2] // TILE_W)[None, :], axis=1)
    offsets = tile_ids - first_tiles
    per_tile = row_counts * col_counts
    within = offsets % per_tile
    return sample_ids, offsets // per_tile, within // col_counts, within % col_counts


def lane_tables():
    third = HEAD_DIM // 6
    part_sizes = (HEAD_DIM - 4 * third, 2 * third, 2 * third)
    part = np.concatenate([np.full(size, at) for at, size in enumerate(part_sizes)])
    pair_at = np.concatenate([np.arange(size) // 2 * 2 for size in part_sizes])
    size_at = np.concatenate([np.full(size, size) for size in part_sizes])
    return part, pair_at.astype(np.float32), size_at.astype(np.float32)


def rotation(frames, bands, columns):
    part, pair_at, size_at = lane_tables()
    inner = jnp.arange(TILE, dtype=jnp.int32)
    tiles = frames.shape[0]
    time_pos = jnp.broadcast_to(frames[:, None], (tiles, TILE)).reshape(-1, 1)
    row_pos = (bands[:, None] * TILE_H + inner[None, :] // TILE_W).reshape(-1, 1)
    col_pos = (columns[:, None] * TILE_W + inner[None, :] % TILE_W).reshape(-1, 1)
    lane_part = jnp.asarray(part, jnp.int32)[None, :]
    position = jnp.where(lane_part == 0, time_pos, jnp.where(lane_part == 1, row_pos, col_pos))
    frequency = 10000.0 ** (-jnp.asarray(pair_at) / jnp.asarray(size_at))
    angles = position.astype(jnp.float32) * frequency[None, :]
    sign = jnp.asarray(np.where(np.arange(HEAD_DIM) % 2 == 0, -1.0, 1.0), jnp.float32)
    return jnp.cos(angles), jnp.sin(angles) * sign[None, :]


def head_sum(partial):
    count = lax.axis_size("head")
    if count & (count - 1):
        return lax.psum(partial, "head")
    step = 1
    while step < count:
        partial = partial + lax.ppermute(partial, "head", [(i, i ^ step) for i in range(count)])
        step *= 2
    return partial


def turn_kernel(x_ref, cos_ref, sin_ref, gain_ref, swapped_gain_ref, o_ref):
    x = x_ref[...]
    row = lax.broadcasted_iota(jnp.int32, (HEAD_DIM, HEAD_DIM), 0)
    col = lax.broadcasted_iota(jnp.int32, (HEAD_DIM, HEAD_DIM), 1)
    exchange = (row == col + 1 - 2 * (col % 2)).astype(jnp.bfloat16)
    swapped = jnp.dot(x, exchange, preferred_element_type=jnp.float32)
    turned = (x.astype(jnp.float32) * gain_ref[...]) * cos_ref[...]
    turned += (swapped * swapped_gain_ref[...]) * sin_ref[...]
    o_ref[...] = turned.astype(jnp.bfloat16)


def turn(field, cosine, sine, gain):
    rows, width = field.shape
    heads = width // HEAD_DIM
    swapped_gain = gain.reshape(-1, 2)[:, ::-1].reshape(1, width)
    column = pl.BlockSpec((rows, HEAD_DIM), lambda h: (0, h))
    table = pl.BlockSpec((rows, HEAD_DIM), lambda h: (0, 0))
    line = pl.BlockSpec((1, HEAD_DIM), lambda h: (0, h))
    return pl.pallas_call(
        turn_kernel,
        grid=(heads,),
        in_specs=[column, table, table, line, line],
        out_specs=column,
        out_shape=jax.ShapeDtypeStruct((rows, width), jnp.bfloat16),
        compiler_params=pltpu.CompilerParams(vmem_limit_bytes=24 * 2**20),
        cost_estimate=pl.CostEstimate(
            flops=2 * rows * width * HEAD_DIM, bytes_accessed=4 * rows * width, transcendentals=0
        ),
    )(field, cosine, sine, gain.reshape(1, width), swapped_gain)


def attend_kernel(meta_ref, q_ref, k_ref, v_ref, kn_ref, vn_ref, tk_ref, tv_ref, *rest):
    o_ref, key_ref, val_ref, s_ref, p_ref = rest[-5:]
    own, near = k_ref.shape[0], kn_ref.shape[0]
    total = own + near + TXT

    @pl.when(pl.program_id(0) == 0)
    def _():
        val_ref[:, HEAD_DIM:] = jnp.ones((total, HEAD_DIM), jnp.bfloat16)

    key_ref[:own, :] = k_ref[...]
    key_ref[own : own + near, :] = kn_ref[...]
    key_ref[own + near :, :] = tk_ref[...]
    val_ref[:own, :HEAD_DIM] = v_ref[...]
    val_ref[own : own + near, :HEAD_DIM] = vn_ref[...]
    val_ref[own + near :, :HEAD_DIM] = tv_ref[...]
    window_tiles = (own + near) // TILE
    key_tiles = total // TILE
    for i in range(FRAME_TILES):
        rows = slice(i * TILE, (i + 1) * TILE)
        s_ref[rows, :] = lax.dot_general(
            q_ref[rows, :],
            key_ref[...],
            (((1,), (1,)), ((), ())),
            preferred_element_type=jnp.float32,
        )
        bias = [
            jnp.where(meta_ref[1 + i * window_tiles + j] == 0, OUT_OF_WINDOW, 0.0)
            for j in range(window_tiles)
        ]
        largest = None
        for j in range(key_tiles):
            part = s_ref[rows, j * TILE : (j + 1) * TILE]
            if j < window_tiles:
                part = part + bias[j]
            largest = part if largest is None else jnp.maximum(largest, part)
        largest = jnp.max(largest, axis=1, keepdims=True)
        for j in range(key_tiles):
            cols = slice(j * TILE, (j + 1) * TILE)
            top = largest - bias[j] if j < window_tiles else largest
            p_ref[rows, cols] = jnp.exp2(s_ref[rows, cols] - top).astype(jnp.bfloat16)
        mixed = jnp.dot(p_ref[rows, :], val_ref[...], preferred_element_type=jnp.float32)
        o_ref[rows, :] = (mixed[:, :HEAD_DIM] / mixed[:, HEAD_DIM:]).astype(jnp.bfloat16)


def attend(meta, q_hat, k_hat, values, near_k, near_v, text, place, first, heads, out=None):
    rows, width = q_hat.shape
    total = rows + FRAME + TXT

    def own(h, meta):
        return (0, first + h)

    frame_block = pl.BlockSpec((FRAME, HEAD_DIM), lambda h, meta: (meta[0], first + h))
    near_spec = pl.BlockSpec((None, FRAME, HEAD_DIM), lambda h, meta: (0, 0, h))
    near_spec_v = pl.BlockSpec(
        (None, FRAME, HEAD_DIM), lambda h, meta: (near_v.shape[0] - 1, 0, h)
    )
    text_specs = [
        pl.BlockSpec((None, None, TXT, HEAD_DIM), lambda h, meta, at=at: (at, place, 0, first + h))
        for at in range(2)
    ]
    in_specs = [
        frame_block,
        pl.BlockSpec((rows, HEAD_DIM), own),
        pl.BlockSpec((rows, HEAD_DIM), own),
        near_spec,
        near_spec_v,
        *text_specs,
    ]
    operands = [q_hat, k_hat, values, near_k, near_v, text, text]
    aliases = {}
    if out is not None:
        in_specs.append(pl.BlockSpec(memory_space=pl.ANY))
        operands.append(out)
        aliases = {len(operands): 0}
    return pl.pallas_call(
        attend_kernel,
        grid_spec=pltpu.PrefetchScalarGridSpec(
            num_scalar_prefetch=1,
            grid=(heads,),
            in_specs=in_specs,
            out_specs=frame_block,
            scratch_shapes=[
                pltpu.VMEM((total, HEAD_DIM), jnp.bfloat16),
                pltpu.VMEM((total, 2 * HEAD_DIM), jnp.bfloat16),
                pltpu.VMEM((FRAME, total), jnp.float32),
                pltpu.VMEM((FRAME, total), jnp.bfloat16),
            ],
        ),
        out_shape=jax.ShapeDtypeStruct((rows, width), jnp.bfloat16),
        input_output_aliases=aliases,
        compiler_params=pltpu.CompilerParams(vmem_limit_bytes=32 * 2**20),
        cost_estimate=pl.CostEstimate(
            flops=heads * FRAME * total * HEAD_DIM * 8,
            bytes_accessed=heads * (2 * total + 2 * FRAME) * HEAD_DIM * 2,
            transcendentals=heads * FRAME * total,
        ),
    )(meta, *operands)


def after(value, *others):
    return lax.optimization_barrier((value, *others))[0]


def local(
    queries, keys, values, query_gain, key_gain, shapes, windows, text_keys, text_values, owner
):
    rows, width = queries.shape
    heads = width // HEAD_DIM
    tiles = rows // TILE
    count = lax.axis_size("seq")
    me = lax.axis_index("seq")
    odd = me % 2
    first_tile = me * tiles
    pair = [(i, i ^ 1) for i in range(count)]
    side = [p for i in range(1, count - 1, 2) for p in ((i, i + 1), (i + 1, i))]
    pair_frame, side_frame = 1 - odd, odd

    chosen = jnp.stack([jnp.take(text_keys, owner, axis=0), jnp.take(text_values, owner, axis=0)])
    both = jnp.concatenate([chosen, lax.ppermute(chosen, "seq", pair)], axis=2)
    pair_values = lax.dynamic_slice_in_dim(values, pair_frame * FRAME, FRAME, 0)[None]
    near_values = lax.ppermute(pair_values, "seq", pair)
    if count <= 8:
        text = jnp.concatenate(
            [both]
            + [
                lax.ppermute(both, "seq", [(i, (i + 2 * k) % count) for i in range(count)])
                for k in range(1, count // 2)
            ],
            axis=2,
        )
    else:
        groups = [list(range(start, count, 2)) for start in range(2)]
        text = lax.all_gather(both, "seq", axis=2, tiled=True, axis_index_groups=groups)

    tile_ids = first_tile + jnp.arange(tiles, dtype=jnp.int32)
    sample_ids, frames, bands, columns = tile_positions(tile_ids, shapes)
    cosine, sine = rotation(frames, bands, columns)
    query_wide = queries.astype(jnp.float32)
    key_wide = keys.astype(jnp.float32)
    squares = head_sum(
        jnp.stack([jnp.sum(query_wide * query_wide, axis=1), jnp.sum(key_wide * key_wide, axis=1)])
    )
    scale = lax.rsqrt(squares / D + EPSILON)
    key_scale = scale[1][:, None]
    query_scale = scale[0][:, None] * (HEAD_DIM**-0.5 * math.log2(math.e))
    k_hat = turn(keys, cosine * key_scale, sine * key_scale, key_gain)
    pair_keys = lax.dynamic_slice_in_dim(k_hat, pair_frame * FRAME, FRAME, 0)[None]
    near_keys = lax.ppermute(pair_keys, "seq", pair)
    q_hat = turn(queries, cosine * query_scale, sine * query_scale, query_gain)

    step = 2 if heads % 2 == 0 else 1
    side_keys = lax.dynamic_slice_in_dim(k_hat, side_frame * FRAME, FRAME, 0)
    side_values = lax.dynamic_slice_in_dim(values, side_frame * FRAME, FRAME, 0)
    arrived = [near_values, near_keys]
    for start in range(0, heads, step):
        cols = slice(start * HEAD_DIM, (start + step) * HEAD_DIM)
        parcel = jnp.stack([side_keys[:, cols], side_values[:, cols]])
        arrived.append(lax.ppermute(after(parcel, arrived[-2]), "seq", side))
    side_parcels = arrived[2:]

    own_ids = tile_ids.reshape(2, FRAME_TILES)
    frame_windows = windows.reshape(2, FRAME_TILES, windows.shape[1])
    frame_samples = sample_ids.reshape(2, FRAME_TILES)[:, 0]
    order = jnp.stack([pair_frame, side_frame])
    slots = jnp.take(frame_samples, order)
    text = jnp.take(text, slots, axis=1)
    before_ids = own_ids[0] - FRAME_TILES
    after_ids = own_ids[1] + FRAME_TILES

    def meta_of(frame):
        near_ids = jnp.where(frame == 0, before_ids, after_ids)
        key_ids = jnp.concatenate([own_ids[0], own_ids[1], near_ids])
        listed = jnp.take(frame_windows, frame, axis=0)
        allowed = jnp.any(listed[:, :, None] == key_ids[None, None, :], axis=1) & (key_ids >= 0)
        return jnp.concatenate([frame[None], allowed.astype(jnp.int32).reshape(-1)])

    out = attend(
        meta_of(pair_frame), q_hat, k_hat, values, near_keys, near_values, text, 0, 0, heads
    )
    meta = meta_of(side_frame)
    for at, parcel in enumerate(side_parcels):
        out = attend(
            meta, q_hat, k_hat, values, parcel, parcel, text, 1, at * step, step, out
        )
    return out


def solution(mesh):
    placed = (
        P("seq", "head"),
        P("seq", "head"),
        P("seq", "head"),
        P("head"),
        P("head"),
        P(),
        P("seq", None),
        P(None, "seq", "head"),
        P(None, "seq", "head"),
        P(),
    )
    return jax.shard_map(
        local, mesh=mesh, in_specs=placed, out_specs=P("seq", "head"), check_vma=False
    )
```

time: 576 us -> 183 us (0.32)
  waiting for transfers between devices: 209 us -> 62.9 us
  local copies, waits for them, and re-layouts: 131 us -> 23.2 us
  matrix products: 97.8 us -> 0 us
  other arithmetic: 106 us -> 16.5 us
  Pallas kernels: 0 us -> 52.1 us
  starting transfers between devices: 6.91 us -> 26.1 us
  between operations: 13.6 us -> 0.43 us
  blocking collectives: 7.08 us -> 0 us
    ppermute x2 -> x13, waiting for transfers between devices: 209 us -> 62.9 us  [the longest x3 42.5 us: local(): lax.ppermute(both, 'seq', [(i, (i + 2 * k) % count) for i in range(count)])]
    dot_general x4 -> x0, matrix products: 97.8 us -> none  [the longest x2 50.4 us: attend(): jnp.einsum('hqk,khd->qhd', weights.astype(jnp.bfloat16), all_values, pref...]
    pallas_call x0 -> x8, Pallas kernels: none -> 52.1 us  [the longest x6 45.7 us: attend(): pl.pallas_call(attend_kernel, grid_spec=pltpu.PrefetchScalarGridSpec(num_...]
    reduce_sum x4 -> x2, other arithmetic: 38 us -> 0.17 us  [the longest x1 0.09 us: tile_positions(): first_tiles = jnp.sum(one_hot * tile_starts[None, :], axis=1)]
    another operation x7 -> x9, other arithmetic: 40.3 us -> 6.46 us  [the longest x5 4.29 us: local(): parcel = jnp.stack([side_keys[:, cols], side_values[:, cols]])]
    dynamic_slice x10 -> x0, local copies, waits for them, and re-layouts: 23.5 us -> none  [the longest x2 19 us: attend(): lax.dynamic_slice_in_dim(extended[0], start_tile * tile_rows, span_tiles...]
    slice x5 -> x2, local copies, waits for them, and re-layouts: 23.4 us -> 0.19 us  [the longest x1 0.11 us: local(): frame_samples = sample_ids.reshape(2, FRAME_TILES)[:, 0]]
    ppermute x2 -> x13, starting transfers between devices: 6.91 us -> 26.1 us  [the longest x5 16.2 us: local(): arrived.append(lax.ppermute(after(parcel, arrived[-2]), 'seq', side))]
  transfers between devices with their start and end apart: 3 -> 13, of which waited for: 2 -> 6; matrix products, arithmetic and copies ran while one was open for 18% -> 18% of each run, Pallas kernels for 0% -> 26%
where the time goes in v1:
time: 183 us; the launch traced here: 181 us
  waiting for transfers between devices  62.9 us (34%)
  Pallas kernels  52.1 us (28%)
  starting transfers between devices  26.1 us (14%)
  local copies, waits for them, and re-layouts  23.2 us (13%)
  other arithmetic  16.5 us (9%)
    pallas_call x6, Pallas kernels, attend(): pl.pallas_call(attend_kernel, grid_spec=pltpu.PrefetchScalarGridSpec(num_...  45.7 us
    ppermute x3, waiting for transfers between devices, local(): lax.ppermute(both, 'seq', [(i, (i + 2 * k) % count) for i in range(count)])  42.5 us
    ppermute x5, starting transfers between devices, local(): arrived.append(lax.ppermute(after(parcel, arrived[-2]), 'seq', side))  16.2 us
    ppermute x1, waiting for transfers between devices, local(): both = jnp.concatenate([chosen, lax.ppermute(chosen, 'seq', pair)], axis=2)  11.4 us
    ppermute x5, waiting for transfers between devices, local(): arrived.append(lax.ppermute(after(parcel, arrived[-2]), 'seq', side))  8.85 us
    unnamed x58, local copies, waits for them, and re-layouts  7.97 us
    pallas_call x2, Pallas kernels, turn(): pl.pallas_call(turn_kernel, grid=(heads,), in_specs=[column, table, table...  6.41 us
    ppermute x3, starting transfers between devices, local(): lax.ppermute(both, 'seq', [(i, (i + 2 * k) % count) for i in range(count)])  4.67 us
  transfers between devices with their start and end apart: 13, of which 6 were waited for; matrix products, arithmetic and copies ran while one was open for 18% of the time, Pallas kernels for 26%

profile of v1, /device:TPU:8, one launch (start us, length us, event | category | flops | bytes accessed | tf_op | source)
XLA Modules:
  0.0 181.1 jit_solution(17299872544558572525)
XLA Ops:
  0.0 2.5 %multiply_reduce_fusion = f32[1024]{0:T(1024)S(1)} fusion(bf16[1024,1280]{1,0:T(8,128)(2,1)} %x_ref.3), kind=kLoop, calls=%fused_computation.4 | loop fusion | flops 3931136 | bytes 2625536 | tf_op jit(solution)/shard_map/reduce_sum | solution.py:248
  3.4 1.1 dynamic-slice_bitcast_fusion.1
  4.5 1.5 collective-permute-start.2
  6.1 1.2 gather_fusion.2
  7.3 2.3 %gather_fusion.3 = bf16[2,32,1280]{2,1,0:T(8,128)(2,1)} fusion(bf16[8,32,1280]{2,1,0:T(8,128)(2,1)} %param.26, s32[1024]{0:T(1024)S(1)} %pad_clamp_fusion.1), kind=kCustom, calls=%fused_computation.1.clone | custom fusion | bytes 327688 | tf_op jit(solution)/shard_map/jit(_take)/gather | solution.py:225
  9.6 1.1 select_bitcast_fusion.1
  10.7 0.7 copy-done.8
  11.4 0.9 pad_maximum_fusion.6
  16.2 1.1 dynamic-slice_bitcast_fusion.2
  17.5 1.6 collective-permute-start.1
  21.3 2.0 %fusion.4 = (f32[1024,128]{1,0:T(8,128)S(1)}, f32[1024,128]{1,0:T(8,128)S(1)}, f32[1024,128]{1,0:T(8,128)S(1)}, f32[1024,128]{1,0:T(8,128)S(1)}) fusion(f32[1024]{0:T(1024)S(1)} %bitcast.86, f32[128]{0:T(128)S(1)} %copy-done.21, f32[128]{0:T(128)S(1)} %copy-done.22, s32[1024]{0:T(1024)S(1)} %add_bitcast_fusion, s32[1024]{0:T(1024)S(1)} %add_bitcast_fusion.1, ...), kind=kLoop, calls=%fused_computation.21 | loop fusion | flops 1179648 | bytes 2118912 | tf_op jit(solution)/shard_map/mul | solution.py:253
  23.4 1.7 copy-done.5
  25.1 3.2 %shard_map.137.k_ref = bf16[1024,1280]{1,0:T(8,128)(2,1)S(1)} custom-call(bf16[1024,1280]{1,0:T(8,128)(2,1)S(1)} %copy-done.5, f32[1024,128]{1,0:T(8,128)S(1)} %get-tuple-element.53.cos_ref, f32[1024,128]{1,0:T(8,128)S(1)} %get-tuple-element.52.sin_ref, f32[1,1280]{1,0:T(1,128)S(1)} %reshape.530.gain_ref, f32[1,1280]{1,0:T(1,128)S(1)} %reshape.532.swapped_gain_ref), custom_call_target="tpu_custom_call" | custom-call | flops 335544320 | bytes 5242880 | tf_op jit(solution)/shard_map/pallas_call | solution.py:95
  28.3 1.2 dynamic-slice_bitcast_fusion
  29.5 1.5 collective-permute-start.10
  31.2 0.9 pad_maximum_fusion.1
  32.0 11.4 %collective-permute-done.6 = bf16[2,2,32,1280]{3,2,1,0:T(8,128)(2,1)} collective-permute-done((bf16[2,2,32,1280]{3,2,1,0:T(8,128)(2,1)}, bf16[2,2,32,1280]{3,2,1,0:T(8,128)(2,1)}, u32[]{:S(2)}, u32[]{:S(2)}) %collective-permute-start.6) | collective-permute-done | bytes 327712 | tf_op jit(solution)/shard_map/ppermute | solution.py:226
  43.5 1.0 pad_maximum_fusion
  44.5 1.6 collective-permute-start.7
  46.1 0.8 pad_maximum_fusion.2
  47.0 0.9 pad_maximum_fusion.3
  47.8 1.0 collective-permute-start.8
  48.8 0.8 pad_maximum_fusion.4
  49.7 3.2 %shard_map.136.q_ref = bf16[1024,1280]{1,0:T(8,128)(2,1)S(1)} custom-call(bf16[1024,1280]{1,0:T(8,128)(2,1)S(1)} %copy-done.7, f32[1024,128]{1,0:T(8,128)S(1)} %get-tuple-element.56.cos_ref, f32[1024,128]{1,0:T(8,128)S(1)} %get-tuple-element.57.sin_ref, f32[1,1280]{1,0:T(1,128)S(1)} %reshape.527.gain_ref, f32[1,1280]{1,0:T(1,128)S(1)} %reshape.529.swapped_gain_ref), custom_call_target="tpu_custom_call" | custom-call | flops 335544320 | bytes 5242880 | tf_op jit(solution)/shard_map/pallas_call | solution.py:95
  52.9 1.5 copy-done.3
  54.4 0.9 pad_maximum_fusion.5
  55.3 2.0 %collective-permute-start.9 = (bf16[2,2,64,1280]{3,2,1,0:T(8,128)(2,1)S(1)}, bf16[2,2,64,1280]{3,2,1,0:T(8,128)(2,1)S(1)}, u32[]{:S(2)}, u32[]{:S(2)}) collective-permute-start(bf16[2,2,64,1280]{3,2,1,0:T(8,128)(2,1)S(1)} %pad_maximum_fusion), channel_id=1, source_target_pairs={{0,24},{4,28},{8,0},{12,4},{16,8},{20,12},{24,16},{28,20},{1,25},{... | collective-permute-start | bytes 1966088 | tf_op jit(solution)/shard_map/ppermute | solution.py:233
  57.3 1.7 constant_dynamic-update-slice_fusion.3
  59.0 30.4 %collective-permute-done.7 = bf16[2,2,64,1280]{3,2,1,0:T(8,128)(2,1)S(1)} collective-permute-done((bf16[2,2,64,1280]{3,2,1,0:T(8,128)(2,1)S(1)}, bf16[2,2,64,1280]{3,2,1,0:T(8,128)(2,1)S(1)}, u32[]{:S(2)}, u32[]{:S(2)}) %collective-permute-start.7) | collective-permute-done | bytes 655392 | tf_op jit(solution)/shard_map/ppermute | solution.py:233
  89.4 0.9 constant_dynamic-update-slice_fusion.2
  90.3 11.3 %collective-permute-done.8 = bf16[2,2,64,1280]{3,2,1,0:T(8,128)(2,1)S(1)} collective-permute-done((bf16[2,2,64,1280]{3,2,1,0:T(8,128)(2,1)S(1)}, bf16[2,2,64,1280]{3,2,1,0:T(8,128)(2,1)S(1)}, u32[]{:S(2)}, u32[]{:S(2)}) %collective-permute-start.8) | collective-permute-done | bytes 655392 | tf_op jit(solution)/shard_map/ppermute | solution.py:233
  101.6 0.9 constant_dynamic-update-slice_fusion.1
  102.5 0.9 collective-permute-done.9
  103.4 0.9 constant_dynamic-update-slice_fusion
  104.3 4.0 %gather_fusion.1 = bf16[2,2,256,1280]{3,2,1,0:T(8,128)(2,1)} fusion(bf16[2,2,256,1280]{3,2,1,0:T(8,128)(2,1)} %constant_dynamic-update-slice_fusion, s32[1024]{0:T(1024)S(1)} %pad_clamp_fusion), kind=kCustom, calls=%fused_computation.3 | custom fusion | bytes 5242888 | tf_op jit(solution)/shard_map/jit(_take)/gather | solution.py:273
  108.3 2.3 %collective-permute-start.3 = (bf16[2,512,256]{2,1,0:T(8,128)(2,1)}, bf16[2,512,256]{2,1,0:T(8,128)(2,1)S(1)}, u32[]{:S(2)}, u32[]{:S(2)}) collective-permute-start(bf16[2,512,256]{2,1,0:T(8,128)(2,1)} %pad_maximum_fusion.3), channel_id=1, source_target_pairs={{4,8},{8,4},{12,16},{16,12},{20,24},{24,20},{5,9},{9,5},{13,17},{1... | collective-permute-start | bytes 1572872 | tf_op jit(solution)/shard_map/ppermute | solution.py:265
  110.6 2.0 %fusion.tk_ref.tv_ref = bf16[2,2,256,1280]{3,2,1,0:T(8,128)(2,1)S(1)} fusion(bf16[2,2,256,1280]{3,2,1,0:T(8,128)(2,1)} %gather_fusion.1, pred[2]{0:T(512)(128)(4,1)S(1)} %compare_and_fusion.1), kind=kLoop, calls=%fused_computation.7 | loop fusion | flops 1310720 | bytes 5242882 | tf_op jit(solution)/shard_map/jit(_take)/select_n | solution.py:273
  112.7 4.8 %collective-permute-start.11 = (bf16[2,512,256]{2,1,0:T(8,128)(2,1)}, bf16[2,512,256]{2,1,0:T(8,128)(2,1)S(1)}, u32[]{:S(2)}, u32[]{:S(2)}) collective-permute-start(bf16[2,512,256]{2,1,0:T(8,128)(2,1)} %pad_maximum_fusion.5), channel_id=1, source_target_pairs={{4,8},{8,4},{12,16},{16,12},{20,24},{24,20},{5,9},{9,5},{13,17},{1... | collective-permute-start | bytes 1572872 | tf_op jit(solution)/shard_map/ppermute | solution.py:265
  117.5 8.8 %collective-permute-done.3.kn_ref.vn_ref = bf16[2,512,256]{2,1,0:T(8,128)(2,1)S(1)} collective-permute-done((bf16[2,512,256]{2,1,0:T(8,128)(2,1)}, bf16[2,512,256]{2,1,0:T(8,128)(2,1)S(1)}, u32[]{:S(2)}, u32[]{:S(2)}) %collective-permute-start.3) | collective-permute-done | bytes 524320 | tf_op jit(solution)/shard_map/ppermute | solution.py:265
  126.3 2.0 %collective-permute-start.4 = (bf16[2,512,256]{2,1,0:T(8,128)(2,1)}, bf16[2,512,256]{2,1,0:T(8,128)(2,1)S(1)}, u32[]{:S(2)}, u32[]{:S(2)}) collective-permute-start(bf16[2,512,256]{2,1,0:T(8,128)(2,1)} %pad_maximum_fusion.2), channel_id=1, source_target_pairs={{4,8},{8,4},{12,16},{16,12},{20,24},{24,20},{5,9},{9,5},{13,17},{1... | collective-permute-start | bytes 1572872 | tf_op jit(solution)/shard_map/ppermute | solution.py:265
  128.3 20.5 %shard_map.138.rest_0_ = bf16[1024,1280]{1,0:T(8,128)(2,1)} custom-call(s32[49]{0:T(128)S(1)} %pad_add_fusion.3.meta_ref, bf16[1024,1280]{1,0:T(8,128)(2,1)S(1)} %copy-done.4, bf16[1024,1280]{1,0:T(8,128)(2,1)S(1)} %shard_map.137.k_ref, bf16[1024,1280]{1,0:T(8,128)(2,1)S(1)} %copy-done.2, bf16[1,512,1280]{2,1,0:T(8,128)(2,1)} %collective-permute-done.10.kn_ref, ...), custom_call_target="tpu_custom_call" | custom-call | flops 9395240960 | bytes 11796480 | tf_op jit(solution)/shard_map/pallas_call | solution.py:182
  148.8 5.0 %collective-permute-start.12 = (bf16[2,512,256]{2,1,0:T(8,128)(2,1)S(1)}, bf16[2,512,256]{2,1,0:T(8,128)(2,1)S(1)}, u32[]{:S(2)}, u32[]{:S(2)}) collective-permute-start(bf16[2,512,256]{2,1,0:T(8,128)(2,1)S(1)} %copy-done.16), channel_id=1, source_target_pairs={{4,8},{8,4},{12,16},{16,12},{20,24},{24,20},{5,9},{9,5},{13,17},{1... | collective-permute-start | bytes 1572872 | tf_op jit(solution)/shard_map/ppermute | solution.py:265
  153.9 5.0 %shard_map.139.rest_0_ = bf16[1024,1280]{1,0:T(8,128)(2,1)} custom-call(s32[49]{0:T(128)S(1)} %pad_add_fusion.1.meta_ref, bf16[1024,1280]{1,0:T(8,128)(2,1)S(1)} %copy-done.4, bf16[1024,1280]{1,0:T(8,128)(2,1)S(1)} %shard_map.137.k_ref, bf16[1024,1280]{1,0:T(8,128)(2,1)S(1)} %copy-done.2, ...), custom_call_target="tpu_custom_call", output_to_operand_aliasing={{}: (8, {})} | custom-call | flops 1879048192 | bytes 2359296 | tf_op jit(solution)/shard_map/pallas_call | solution.py:182
  158.9 2.0 %collective-permute-start.5 = (bf16[2,512,256]{2,1,0:T(8,128)(2,1)S(1)}, bf16[2,512,256]{2,1,0:T(8,128)(2,1)S(1)}, u32[]{:S(2)}, u32[]{:S(2)}) collective-permute-start(bf16[2,512,256]{2,1,0:T(8,128)(2,1)S(1)} %copy-done.15), channel_id=1, source_target_pairs={{4,8},{8,4},{12,16},{16,12},{20,24},{24,20},{5,9},{9,5},{13,17},{1... | collective-permute-start | bytes 1572872 | tf_op jit(solution)/shard_map/ppermute | solution.py:265
  160.9 5.0 %shard_map.140.rest_0_ = bf16[1024,1280]{1,0:T(8,128)(2,1)} custom-call(s32[49]{0:T(128)S(1)} %pad_add_fusion.1.meta_ref, bf16[1024,1280]{1,0:T(8,128)(2,1)S(1)} %copy-done.4, bf16[1024,1280]{1,0:T(8,128)(2,1)S(1)} %shard_map.137.k_ref, bf16[1024,1280]{1,0:T(8,128)(2,1)S(1)} %copy-done.2, ...), custom_call_target="tpu_custom_call", output_to_operand_aliasing={{}: (8, {})} | custom-call | flops 1879048192 | bytes 2359296 | tf_op jit(solution)/shard_map/pallas_call | solution.py:182
  166.0 5.0 %shard_map.141.rest_0_ = bf16[1024,1280]{1,0:T(8,128)(2,1)} custom-call(s32[49]{0:T(128)S(1)} %pad_add_fusion.1.meta_ref, bf16[1024,1280]{1,0:T(8,128)(2,1)S(1)} %copy-done.4, bf16[1024,1280]{1,0:T(8,128)(2,1)S(1)} %shard_map.137.k_ref, bf16[1024,1280]{1,0:T(8,128)(2,1)S(1)} %copy-done.2, ...), custom_call_target="tpu_custom_call", output_to_operand_aliasing={{}: (8, {})} | custom-call | flops 1879048192 | bytes 2359296 | tf_op jit(solution)/shard_map/pallas_call | solution.py:182
  171.0 5.0 %shard_map.142.rest_0_ = bf16[1024,1280]{1,0:T(8,128)(2,1)} custom-call(s32[49]{0:T(128)S(1)} %pad_add_fusion.1.meta_ref, bf16[1024,1280]{1,0:T(8,128)(2,1)S(1)} %copy-done.4, bf16[1024,1280]{1,0:T(8,128)(2,1)S(1)} %shard_map.137.k_ref, bf16[1024,1280]{1,0:T(8,128)(2,1)S(1)} %copy-done.2, ...), custom_call_target="tpu_custom_call", output_to_operand_aliasing={{}: (8, {})} | custom-call | flops 1879048192 | bytes 2359296 | tf_op jit(solution)/shard_map/pallas_call | solution.py:182
  176.1 5.0 %shard_map.143 = bf16[1024,1280]{1,0:T(8,128)(2,1)} custom-call(s32[49]{0:T(128)S(1)} %pad_add_fusion.1.meta_ref, bf16[1024,1280]{1,0:T(8,128)(2,1)S(1)} %copy-done.4, bf16[1024,1280]{1,0:T(8,128)(2,1)S(1)} %shard_map.137.k_ref, bf16[1024,1280]{1,0:T(8,128)(2,1)S(1)} %copy-done.2, ...), custom_call_target="tpu_custom_call", output_to_operand_aliasing={{}: (8, {})} | custom-call | flops 1879048192 | bytes 2359296 | tf_op jit(solution)/shard_map/pallas_call | solution.py:182
  (111 shorter events, 7.3 us)
Async XLA Ops:
  0.0 6.1 %copy-start = (bf16[8,32,1280]{2,1,0:T(8,128)(2,1)S(1)}, bf16[8,32,1280]{2,1,0:T(8,128)(2,1)}, u32[]{:S(2)}) copy-start(bf16[8,32,1280]{2,1,0:T(8,128)(2,1)} %param.25) | copy-start | bytes 1966084
  0.0 2.6 %copy-start.6 = (bf16[1024,1280]{1,0:T(8,128)(2,1)S(1)}, bf16[1024,1280]{1,0:T(8,128)(2,1)}, u32[]{:S(2)}) copy-start(bf16[1024,1280]{1,0:T(8,128)(2,1)} %x_ref.2) | copy-start | bytes 7864324
  0.0 3.4 %copy-start.1 = (bf16[1024,1280]{1,0:T(8,128)(2,1)S(1)}, bf16[1024,1280]{1,0:T(8,128)(2,1)}, u32[]{:S(2)}) copy-start(bf16[1024,1280]{1,0:T(8,128)(2,1)} %v_ref.11) | copy-start | bytes 7864324
  2.6 3.4 %copy-start.25 = (s32[2]{0:T(128)S(1)}, s32[2]{0:T(128)}, u32[]{:S(2)}) copy-start(s32[2]{0:T(128)} %param.27) | copy-start | bytes 28
  3.2 9.8 %copy-start.20 = (s32[8,27]{1,0:T(8,128)S(1)}, s32[8,27]{1,0:T(8,128)}, u32[]{:S(2)}) copy-start(s32[8,27]{1,0:T(8,128)} %param.24) | copy-start | bytes 2596
  3.2 10.5 %copy-start.19 = (s32[2,3]{1,0:T(2,128)S(1)}, s32[2,3]{1,0:T(2,128)}, u32[]{:S(2)}) copy-start(s32[2,3]{1,0:T(2,128)} %param.23) | copy-start | bytes 76
  3.2 14.3 %collective-permute-start = (f32[2,1024]{1,0:T(2,128)S(1)}, f32[2,1024]{1,0:T(2,128)S(1)}, u32[]{:S(2)}, u32[]{:S(2)}) collective-permute-start(f32[2,1024]{1,0:T(2,128)S(1)} %pad_maximum_fusion.7), channel_id=1, source_target_pairs={{0,1},{1,0},{2,3},{3,2},{4,5},{5,4},{6,7},{7,6},{8,9},{9,8},{10,11... | collective-permute-start | bytes 24584 | tf_op jit(solution)/shard_map/ppermute | solution.py:72
  4.5 103.7 %collective-permute-start.2 = (bf16[1,512,1280]{2,1,0:T(8,128)(2,1)}, bf16[1,512,1280]{2,1,0:T(8,128)(2,1)}, u32[]{:S(2)}, u32[]{:S(2)}) collective-permute-start(bf16[1,512,1280]{2,1,0:T(8,128)(2,1)} %dynamic-slice_bitcast_fusion.1), channel_id=1, source_target_pairs={{0,4},{4,0},{8,12},{12,8},{16,20},{20,16},{24,28},{28,24},{1,5},{5... | collective-permute-start | bytes 3932168 | tf_op jit(solution)/shard_map/ppermute | solution.py:228
  7.3 11.9 %copy-start.17 = (f32[1280]{0:T(1024)S(1)}, f32[1280]{0:T(1024)}, u32[]{:S(2)}) copy-start(f32[1280]{0:T(1024)} %param.21) | copy-start | bytes 15364
  9.6 9.9 %copy-start.18 = (f32[1280]{0:T(1024)S(1)}, f32[1280]{0:T(1024)}, u32[]{:S(2)}) copy-start(f32[1280]{0:T(1024)} %param.22) | copy-start | bytes 15364
  10.7 0.7 copy-start.8
  12.3 31.2 %collective-permute-start.6 = (bf16[2,2,32,1280]{3,2,1,0:T(8,128)(2,1)}, bf16[2,2,32,1280]{3,2,1,0:T(8,128)(2,1)}, u32[]{:S(2)}, u32[]{:S(2)}) collective-permute-start(bf16[2,2,32,1280]{3,2,1,0:T(8,128)(2,1)} %get-tuple-element.50), channel_id=1, source_target_pairs={{0,4},{4,0},{8,12},{12,8},{16,20},{20,16},{24,28},{28,24},{1,5},{5... | collective-permute-start | bytes 983048 | tf_op jit(solution)/shard_map/ppermute | solution.py:226
  16.2 5.1 %copy-start.21 = (f32[128]{0:T(128)S(1)}, f32[128]{0:T(128)}, u32[]{:S(2)}) copy-start(f32[128]{0:T(128)} %constant.178.clone) | copy-start | bytes 1540
  16.2 5.1 %copy-start.22 = (f32[128]{0:T(128)S(1)}, f32[128]{0:T(128)}, u32[]{:S(2)}) copy-start(f32[128]{0:T(128)} %constant.203) | copy-start | bytes 1540
  16.2 5.1 %copy-start.23 = (pred[128]{0:T(512)(128)(4,1)S(1)}, pred[128]{0:T(512)(128)(4,1)}, u32[]{:S(2)}) copy-start(pred[128]{0:T(512)(128)(4,1)} %constant.200) | copy-start | bytes 388
  16.2 5.1 %copy-start.24 = (pred[128]{0:T(512)(128)(4,1)S(1)}, pred[128]{0:T(512)(128)(4,1)}, u32[]{:S(2)}) copy-start(pred[128]{0:T(512)(128)(4,1)} %constant.199) | copy-start | bytes 388
  17.5 3.7 %collective-permute-start.1 = (f32[2,1024]{1,0:T(2,128)S(1)}, f32[2,1024]{1,0:T(2,128)S(1)}, u32[]{:S(2)}, u32[]{:S(2)}) collective-permute-start(f32[2,1024]{1,0:T(2,128)S(1)} %fusion.11), channel_id=1, source_target_pairs={{0,2},{1,3},{2,0},{3,1},{4,6},{5,7},{6,4},{7,5},{8,10},{9,11},{10,... | collective-permute-start | bytes 24584 | tf_op jit(solution)/shard_map/ppermute | solution.py:72
  23.4 1.7 copy-start.5
  28.3 2.8 %copy-start.14 = (bf16[1,512,256]{2,1,0:T(8,128)(2,1)S(1)}, bf16[1,512,256]{2,1,0:T(8,128)(2,1)}, u32[]{:S(2)}) copy-start(bf16[1,512,256]{2,1,0:T(8,128)(2,1)} %get-tuple-element.49) | copy-start | bytes 786436
  28.3 15.1 %copy-start.9 = (bf16[1,2,32,1280]{3,2,1,0:T(8,128)(2,1)S(1)}, bf16[1,2,32,1280]{3,2,1,0:T(8,128)(2,1)}, u32[]{:S(2)}) copy-start(bf16[1,2,32,1280]{3,2,1,0:T(8,128)(2,1)} %copy-done.8) | copy-start | bytes 491524
  29.5 16.6 %copy-start.13 = (bf16[1,512,256]{2,1,0:T(8,128)(2,1)S(1)}, bf16[1,512,256]{2,1,0:T(8,128)(2,1)}, u32[]{:S(2)}) copy-start(bf16[1,512,256]{2,1,0:T(8,128)(2,1)} %get-tuple-element.48) | copy-start | bytes 786436
  29.5 17.4 %copy-start.12 = (bf16[1,512,256]{2,1,0:T(8,128)(2,1)S(1)}, bf16[1,512,256]{2,1,0:T(8,128)(2,1)}, u32[]{:S(2)}) copy-start(bf16[1,512,256]{2,1,0:T(8,128)(2,1)} %get-tuple-element.47) | copy-start | bytes 786436
  29.5 83.1 %collective-permute-start.10 = (bf16[1,512,1280]{2,1,0:T(8,128)(2,1)}, bf16[1,512,1280]{2,1,0:T(8,128)(2,1)}, u32[]{:S(2)}, u32[]{:S(2)}) collective-permute-start(bf16[1,512,1280]{2,1,0:T(8,128)(2,1)} %dynamic-slice_bitcast_fusion), channel_id=1, source_target_pairs={{0,4},{4,0},{8,12},{12,8},{16,20},{20,16},{24,28},{28,24},{1,5},{5... | collective-permute-start | bytes 3932168 | tf_op jit(solution)/shard_map/ppermute | solution.py:255
  31.2 17.7 %copy-start.11 = (bf16[1,512,256]{2,1,0:T(8,128)(2,1)S(1)}, bf16[1,512,256]{2,1,0:T(8,128)(2,1)}, u32[]{:S(2)}) copy-start(bf16[1,512,256]{2,1,0:T(8,128)(2,1)} %get-tuple-element.46) | copy-start | bytes 786436
  31.2 18.5 %copy-start.7 = (bf16[1024,1280]{1,0:T(8,128)(2,1)S(1)}, bf16[1024,1280]{1,0:T(8,128)(2,1)}, u32[]{:S(2)}) copy-start(bf16[1024,1280]{1,0:T(8,128)(2,1)} %x_ref.2) | copy-start | bytes 7864324
  44.5 44.9 %collective-permute-start.7 = (bf16[2,2,64,1280]{3,2,1,0:T(8,128)(2,1)S(1)}, bf16[2,2,64,1280]{3,2,1,0:T(8,128)(2,1)S(1)}, u32[]{:S(2)}, u32[]{:S(2)}) collective-permute-start(bf16[2,2,64,1280]{3,2,1,0:T(8,128)(2,1)S(1)} %pad_maximum_fusion), channel_id=1, source_target_pairs={{0,8},{4,12},{8,16},{12,20},{16,24},{20,28},{24,0},{28,4},{1,9},{5... | collective-permute-start | bytes 1966088 | tf_op jit(solution)/shard_map/ppermute | solution.py:233
  47.8 53.7 %collective-permute-start.8 = (bf16[2,2,64,1280]{3,2,1,0:T(8,128)(2,1)S(1)}, bf16[2,2,64,1280]{3,2,1,0:T(8,128)(2,1)S(1)}, u32[]{:S(2)}, u32[]{:S(2)}) collective-permute-start(bf16[2,2,64,1280]{3,2,1,0:T(8,128)(2,1)S(1)} %pad_maximum_fusion), channel_id=1, source_target_pairs={{0,16},{4,20},{8,24},{12,28},{16,0},{20,4},{24,8},{28,12},{1,17},{... | collective-permute-start | bytes 1966088 | tf_op jit(solution)/shard_map/ppermute | solution.py:233
  49.7 4.7 %copy-start.10 = (bf16[1,512,256]{2,1,0:T(8,128)(2,1)S(1)}, bf16[1,512,256]{2,1,0:T(8,128)(2,1)}, u32[]{:S(2)}) copy-start(bf16[1,512,256]{2,1,0:T(8,128)(2,1)} %get-tuple-element.45) | copy-start | bytes 786436
  52.9 1.5 copy-start.3
  55.3 48.1 %collective-permute-start.9 = (bf16[2,2,64,1280]{3,2,1,0:T(8,128)(2,1)S(1)}, bf16[2,2,64,1280]{3,2,1,0:T(8,128)(2,1)S(1)}, u32[]{:S(2)}, u32[]{:S(2)}) collective-permute-start(bf16[2,2,64,1280]{3,2,1,0:T(8,128)(2,1)S(1)} %pad_maximum_fusion), channel_id=1, source_target_pairs={{0,24},{4,28},{8,0},{12,4},{16,8},{20,12},{24,16},{28,20},{1,25},{... | collective-permute-start | bytes 1966088 | tf_op jit(solution)/shard_map/ppermute | solution.py:233
  108.3 20.1 %copy-start.2 = (bf16[1024,1280]{1,0:T(8,128)(2,1)S(1)}, bf16[1024,1280]{1,0:T(8,128)(2,1)}, u32[]{:S(2)}) copy-start(bf16[1024,1280]{1,0:T(8,128)(2,1)} %v_ref.11) | copy-start | bytes 7864324
  108.3 20.1 %copy-start.4 = (bf16[1024,1280]{1,0:T(8,128)(2,1)S(1)}, bf16[1024,1280]{1,0:T(8,128)(2,1)}, u32[]{:S(2)}) copy-start(bf16[1024,1280]{1,0:T(8,128)(2,1)} %copy-done.3) | copy-start | bytes 7864324
  108.3 18.0 %collective-permute-start.3 = (bf16[2,512,256]{2,1,0:T(8,128)(2,1)}, bf16[2,512,256]{2,1,0:T(8,128)(2,1)S(1)}, u32[]{:S(2)}, u32[]{:S(2)}) collective-permute-start(bf16[2,512,256]{2,1,0:T(8,128)(2,1)} %pad_maximum_fusion.3), channel_id=1, source_target_pairs={{4,8},{8,4},{12,16},{16,12},{20,24},{24,20},{5,9},{9,5},{13,17},{1... | collective-permute-start | bytes 1572872 | tf_op jit(solution)/shard_map/ppermute | solution.py:265
  112.6 36.2 %copy-start.16 = (bf16[2,512,256]{2,1,0:T(8,128)(2,1)S(1)}, bf16[2,512,256]{2,1,0:T(8,128)(2,1)}, u32[]{:S(2)}) copy-start(bf16[2,512,256]{2,1,0:T(8,128)(2,1)} %pad_maximum_fusion.4) | copy-start | bytes 1572868
  112.7 36.2 %collective-permute-start.11 = (bf16[2,512,256]{2,1,0:T(8,128)(2,1)}, bf16[2,512,256]{2,1,0:T(8,128)(2,1)S(1)}, u32[]{:S(2)}, u32[]{:S(2)}) collective-permute-start(bf16[2,512,256]{2,1,0:T(8,128)(2,1)} %pad_maximum_fusion.5), channel_id=1, source_target_pairs={{4,8},{8,4},{12,16},{16,12},{20,24},{24,20},{5,9},{9,5},{13,17},{1... | collective-permute-start | bytes 1572872 | tf_op jit(solution)/shard_map/ppermute | solution.py:265
  126.3 32.6 %collective-permute-start.4 = (bf16[2,512,256]{2,1,0:T(8,128)(2,1)}, bf16[2,512,256]{2,1,0:T(8,128)(2,1)S(1)}, u32[]{:S(2)}, u32[]{:S(2)}) collective-permute-start(bf16[2,512,256]{2,1,0:T(8,128)(2,1)} %pad_maximum_fusion.2), channel_id=1, source_target_pairs={{4,8},{8,4},{12,16},{16,12},{20,24},{24,20},{5,9},{9,5},{13,17},{1... | collective-permute-start | bytes 1572872 | tf_op jit(solution)/shard_map/ppermute | solution.py:265
  148.8 10.1 %copy-start.15 = (bf16[2,512,256]{2,1,0:T(8,128)(2,1)S(1)}, bf16[2,512,256]{2,1,0:T(8,128)(2,1)}, u32[]{:S(2)}) copy-start(bf16[2,512,256]{2,1,0:T(8,128)(2,1)} %pad_maximum_fusion.1) | copy-start | bytes 1572868
  148.8 22.2 %collective-permute-start.12 = (bf16[2,512,256]{2,1,0:T(8,128)(2,1)S(1)}, bf16[2,512,256]{2,1,0:T(8,128)(2,1)S(1)}, u32[]{:S(2)}, u32[]{:S(2)}) collective-permute-start(bf16[2,512,256]{2,1,0:T(8,128)(2,1)S(1)} %copy-done.16), channel_id=1, source_target_pairs={{4,8},{8,4},{12,16},{16,12},{20,24},{24,20},{5,9},{9,5},{13,17},{1... | collective-permute-start | bytes 1572872 | tf_op jit(solution)/shard_map/ppermute | solution.py:265
  158.9 17.1 %collective-permute-start.5 = (bf16[2,512,256]{2,1,0:T(8,128)(2,1)S(1)}, bf16[2,512,256]{2,1,0:T(8,128)(2,1)S(1)}, u32[]{:S(2)}, u32[]{:S(2)}) collective-permute-start(bf16[2,512,256]{2,1,0:T(8,128)(2,1)S(1)} %copy-done.15), channel_id=1, source_target_pairs={{4,8},{8,4},{12,16},{16,12},{20,24},{24,20},{5,9},{9,5},{13,17},{1... | collective-permute-start | bytes 1572872 | tf_op jit(solution)/shard_map/ppermute | solution.py:265

commit v2 on v1

v2 whole, which is shorter than its diff:
```python
import functools
import math

import jax
import jax.numpy as jnp
import numpy as np
from jax import lax
from jax.experimental import pallas as pl
from jax.experimental.pallas import tpu as pltpu
from jax.sharding import PartitionSpec as P

HEAD_DIM = 128
D = 5120
TILE_H = 8
TILE_W = 16
TILE = 128
FRAME_TILES = 4
FRAME = FRAME_TILES * TILE
TXT = 256
WIN = 27
EPSILON = 1e-06
OUT_OF_WINDOW = -1e30
SMALL = pl.CostEstimate(flops=1000, bytes_accessed=1000, transcendentals=0)


def cost(heads, rows, keys):
    return pl.CostEstimate(
        flops=8 * heads * rows * keys * HEAD_DIM,
        bytes_accessed=6 * heads * rows * keys,
        transcendentals=heads * rows * keys,
    )


def lane_tables():
    third = HEAD_DIM // 6
    part_sizes = (HEAD_DIM - 4 * third, 2 * third, 2 * third)
    part = np.concatenate([np.full(size, at) for at, size in enumerate(part_sizes)])
    pair_at = np.concatenate([np.arange(size) // 2 * 2 for size in part_sizes])
    size_at = np.concatenate([np.full(size, size) for size in part_sizes])
    frequency = 10000.0 ** (-jnp.asarray(pair_at, jnp.float32) / jnp.asarray(size_at, jnp.float32))
    return jnp.asarray(part, jnp.int32)[None, :], frequency[None, :]


def plan_kernel(samples, me_ref, shapes_ref, windows_ref, place_ref, own_ref, pair_ref, side_ref):
    me = me_ref[0]
    tiles = 2 * FRAME_TILES
    first = me * tiles
    odd = lax.rem(me, 2)
    narrow = []
    for f in range(2):
        frame_at = first + f * FRAME_TILES
        start, own_start, sample = 0, 0, 0
        single = shapes_ref[2] == TILE_W
        for s in range(samples):
            if s:
                inside = frame_at >= start
                sample = jnp.where(inside, s, sample)
                own_start = jnp.where(inside, start, own_start)
                single = jnp.where(inside, shapes_ref[3 * s + 2] == TILE_W, single)
            start = start + FRAME_TILES * shapes_ref[3 * s]
        narrow.append(single)
        moment = (frame_at - own_start) // FRAME_TILES
        for a in range(FRAME_TILES):
            at = 3 * (f * FRAME_TILES + a)
            place_ref[at] = moment
            place_ref[at + 1] = jnp.where(single, a, a // 2)
            place_ref[at + 2] = jnp.where(single, 0, a % 2)
        is_pair = odd == 1 - f
        for ref, wanted in ((pair_ref, is_pair), (side_ref, jnp.logical_not(is_pair))):

            @pl.when(wanted)
            def _(ref=ref, f=f, sample=sample):
                ref[0] = f
                ref[1] = sample

    def flag(f, a, step, b):
        tall = (step + 1) * 9 + (b - a + 1) * 3 + 1
        square = (step + 1) * 9 + (b // 2 - a // 2 + 1) * 3 + b % 2 - a % 2 + 1
        row = (f * FRAME_TILES + a) * WIN
        key = first + (f + step) * FRAME_TILES + b
        if abs(b - a) > 1:
            found = jnp.logical_and(jnp.logical_not(narrow[f]), windows_ref[row + square] == key)
        else:
            found = windows_ref[row + jnp.where(narrow[f], tall, square)] == key
        return jnp.logical_and(found, key >= 0).astype(jnp.int32)

    for f in range(2):
        near_step = 2 * f - 1
        near = [flag(f, a, near_step, b) for a in range(FRAME_TILES) for b in range(FRAME_TILES)]
        is_pair = odd == 1 - f
        for ref, wanted in ((pair_ref, is_pair), (side_ref, jnp.logical_not(is_pair))):

            @pl.when(wanted)
            def _(ref=ref, near=near):
                for at, value in enumerate(near):
                    ref[2 + at] = value

        for a in range(FRAME_TILES):
            for g in range(2):
                for b in range(FRAME_TILES):
                    at = (f * FRAME_TILES + a) * tiles + g * FRAME_TILES + b
                    own_ref[at] = flag(f, a, g - f, b)


def plan(me, shapes, windows):
    samples = shapes.shape[0]
    tiles = 2 * FRAME_TILES
    smem = pl.BlockSpec(memory_space=pltpu.SMEM)
    sizes = (3 * tiles, tiles * tiles, 2 + FRAME_TILES**2, 2 + FRAME_TILES**2)
    return pl.pallas_call(
        functools.partial(plan_kernel, samples),
        in_specs=[smem] * 3,
        out_specs=[smem] * 4,
        out_shape=[jax.ShapeDtypeStruct((size,), jnp.int32) for size in sizes],
        cost_estimate=SMALL,
    )(me.reshape(1), shapes.reshape(-1), windows.reshape(-1))


def head_sum(partial):
    count = lax.axis_size("head")
    if count & (count - 1):
        return lax.psum(partial, "head")
    step = 1
    while step < count:
        partial = partial + lax.ppermute(partial, "head", [(i, i ^ step) for i in range(count)])
        step *= 2
    return partial


def exchange_pairs(row):
    lane = lax.broadcasted_iota(jnp.int32, row.shape, 1)
    return jnp.where(lane % 2 == 0, pltpu.roll(row, HEAD_DIM - 1, 1), pltpu.roll(row, 1, 1))


def turn_kernel(place_ref, part_ref, frequency_ref, squares_ref, *refs):
    fields, gains, outs, tables = refs[:2], refs[2:4], refs[4:6], refs[6:]
    rows, width = fields[0].shape

    @pl.when(pl.program_id(0) == 0)
    def _():
        token = lax.broadcasted_iota(jnp.int32, (TILE, HEAD_DIM), 0)
        lane = lax.broadcasted_iota(jnp.int32, (TILE, HEAD_DIM), 1)
        part = part_ref[...]
        for i in range(rows // TILE):
            time_pos, band, column = (place_ref[3 * i + axis] for axis in range(3))
            row_pos = band * TILE_H + token // TILE_W
            col_pos = column * TILE_W + token % TILE_W
            position = jnp.where(part == 0, time_pos, jnp.where(part == 1, row_pos, col_pos))
            angles = position.astype(jnp.float32) * frequency_ref[...]
            cosine = jnp.cos(angles)
            sine = jnp.sin(angles) * jnp.where(lane % 2 == 0, -1.0, 1.0)
            at = slice(i * TILE, (i + 1) * TILE)
            for n, factor in enumerate((HEAD_DIM**-0.5 * math.log2(math.e), 1.0)):
                scale = lax.rsqrt(squares_ref[n : n + 1, at] / D + EPSILON) * factor
                scale = jnp.transpose(jnp.broadcast_to(scale, (TILE, HEAD_DIM)))
                tables[2 * n][at, :] = cosine * scale
                tables[2 * n + 1][at, :] = sine * scale

    row = lax.broadcasted_iota(jnp.int32, (HEAD_DIM, HEAD_DIM), 0)
    col = lax.broadcasted_iota(jnp.int32, (HEAD_DIM, HEAD_DIM), 1)
    exchange = (row == col + 1 - 2 * (col % 2)).astype(jnp.bfloat16)
    for n in range(2):
        for u in range(width // HEAD_DIM):
            cols = slice(u * HEAD_DIM, (u + 1) * HEAD_DIM)
            x = fields[n][:, cols]
            gain = jnp.broadcast_to(gains[n][:, cols], (8, HEAD_DIM))
            swapped = jnp.dot(x, exchange, preferred_element_type=jnp.float32)
            turned = (x.astype(jnp.float32) * gain[:1]) * tables[2 * n][...]
            turned += (swapped * exchange_pairs(gain)[:1]) * tables[2 * n + 1][...]
            outs[n][:, cols] = turned.astype(jnp.bfloat16)


def turn(place, squares, queries, keys, query_gain, key_gain):
    rows, width = queries.shape
    heads = width // HEAD_DIM
    step = 2 - heads % 2
    part, frequency = lane_tables()
    column = pl.BlockSpec((rows, step * HEAD_DIM), lambda h, place: (0, h))
    line = pl.BlockSpec((1, step * HEAD_DIM), lambda h, place: (0, h))
    lanes = pl.BlockSpec((1, HEAD_DIM), lambda h, place: (0, 0))
    whole = pl.BlockSpec((2, rows), lambda h, place: (0, 0))
    return pl.pallas_call(
        turn_kernel,
        grid_spec=pltpu.PrefetchScalarGridSpec(
            num_scalar_prefetch=1,
            grid=(heads // step,),
            in_specs=[lanes, lanes, whole, column, column, line, line],
            out_specs=[column, column],
            scratch_shapes=[pltpu.VMEM((rows, HEAD_DIM), jnp.float32) for _ in range(4)],
        ),
        out_shape=[jax.ShapeDtypeStruct((rows, width), jnp.bfloat16)] * 2,
        compiler_params=pltpu.CompilerParams(vmem_limit_bytes=24 * 2**20),
        cost_estimate=SMALL,
    )(
        place,
        part,
        frequency,
        squares,
        queries,
        keys,
        query_gain.reshape(1, width),
        key_gain.reshape(1, width),
    )


def choose_kernel(owner_ref, keys_ref, values_ref, o_ref):
    o_ref[0] = keys_ref[...]
    o_ref[1] = values_ref[...]


def choose(owner, text_keys, text_values):
    panels, rows, width = text_keys.shape
    samples = owner.shape[0]
    panel = pl.BlockSpec((None, rows, width), lambda s, owner: (owner[s], 0, 0))
    return pl.pallas_call(
        choose_kernel,
        grid_spec=pltpu.PrefetchScalarGridSpec(
            num_scalar_prefetch=1,
            grid=(samples,),
            in_specs=[panel, panel],
            out_specs=pl.BlockSpec((2, None, rows, width), lambda s, owner: (0, s, 0, 0)),
        ),
        out_shape=jax.ShapeDtypeStruct((2, samples, rows, width), text_keys.dtype),
        cost_estimate=SMALL,
    )(owner, text_keys, text_values)


def attend_blocks(heads, tiles, query, keys, bias, val_ref, s_ref, p_ref, floor_of, finish):
    def score(u, i):
        rows = slice(i * TILE, (i + 1) * TILE)
        s_ref[u, rows, :] = lax.dot_general(
            query(u, rows),
            keys(u),
            (((1,), (1,)), ((), ())),
            preferred_element_type=jnp.float32,
        )

    def weigh(u, i):
        rows = slice(i * TILE, (i + 1) * TILE)
        largest = None
        for j in range(s_ref.shape[2] // TILE):
            part = s_ref[u, rows, j * TILE : (j + 1) * TILE]
            if j < len(bias[i]):
                part = part + bias[i][j]
            largest = part if largest is None else jnp.maximum(largest, part)
        largest = jnp.max(largest, axis=1, keepdims=True)
        floor = floor_of(u, rows)
        if floor is None:
            largest = jnp.broadcast_to(largest, (TILE, HEAD_DIM))
        else:
            largest = jnp.maximum(largest, floor)
        for j in range(s_ref.shape[2] // TILE):
            cols = slice(j * TILE, (j + 1) * TILE)
            top = largest - bias[i][j] if j < len(bias[i]) else largest
            p_ref[u, rows, cols] = jnp.exp2(s_ref[u, rows, cols] - top).astype(jnp.bfloat16)
        return largest

    def mix(u, i, largest):
        rows = slice(i * TILE, (i + 1) * TILE)
        sums = jnp.dot(p_ref[u, rows, :], val_ref[u], preferred_element_type=jnp.float32)
        finish(u, rows, sums, largest)

    blocks = [(u, i) for i in range(tiles) for u in range(heads)]
    score(*blocks[0])
    waiting = None
    for at, block in enumerate(blocks):
        if at + 1 < len(blocks):
            score(*blocks[at + 1])
        largest = weigh(*block)
        if waiting is not None:
            mix(*waiting)
        waiting = (*block, largest)
    mix(*waiting)


def bias_of(meta_ref, at, tiles):
    return [jnp.where(meta_ref[at + j] == 0, OUT_OF_WINDOW, 0.0) for j in range(tiles)]


def head_cols(u):
    return slice(u * HEAD_DIM, (u + 1) * HEAD_DIM)


def ones_once(val_ref):
    @pl.when(pl.program_id(0) == 0)
    def _():
        for u in range(val_ref.shape[0]):
            val_ref[u, :, HEAD_DIM:] = jnp.ones(val_ref.shape[1:2] + (HEAD_DIM,), jnp.bfloat16)


def own_kernel(meta_ref, q_ref, k_ref, v_ref, *rest):
    o_ref, val_ref, s_ref, p_ref = rest[-4:]
    tiles = k_ref.shape[0] // TILE
    heads = val_ref.shape[0]
    ones_once(val_ref)
    for u in range(heads):
        val_ref[u, :, :HEAD_DIM] = v_ref[:, head_cols(u)]

    def finish(u, rows, sums, largest):
        weight = sums[:, HEAD_DIM:]
        o_ref[rows, head_cols(2 * u)] = sums[:, :HEAD_DIM] / weight
        o_ref[rows, head_cols(2 * u + 1)] = largest + jnp.log2(weight)

    attend_blocks(
        heads,
        tiles,
        lambda u, rows: q_ref[rows, head_cols(u)],
        lambda u: k_ref[:, head_cols(u)],
        [bias_of(meta_ref, i * tiles, tiles) for i in range(tiles)],
        val_ref,
        s_ref,
        p_ref,
        lambda u, rows: None,
        finish,
    )


def attend_own(flags, q_hat, k_hat, values, first, heads, out=None):
    rows, width = q_hat.shape
    step = 1 if heads % 2 or first % 2 else 2
    wide = step * HEAD_DIM
    column = pl.BlockSpec((rows, wide), lambda h, flags: (0, first // step + h))
    operands, in_specs, aliases = [q_hat, k_hat, values], [column] * 3, {}
    if out is not None:
        in_specs.append(pl.BlockSpec(memory_space=pl.ANY))
        operands.append(out)
        aliases = {len(operands): 0}
    return pl.pallas_call(
        own_kernel,
        grid_spec=pltpu.PrefetchScalarGridSpec(
            num_scalar_prefetch=1,
            grid=(heads // step,),
            in_specs=in_specs,
            out_specs=pl.BlockSpec((rows, 2 * wide), lambda h, flags: (0, first // step + h)),
            scratch_shapes=[
                pltpu.VMEM((step, rows, 2 * HEAD_DIM), jnp.bfloat16),
                pltpu.VMEM((step, rows, rows), jnp.float32),
                pltpu.VMEM((step, rows, rows), jnp.bfloat16),
            ],
        ),
        out_shape=jax.ShapeDtypeStruct((rows, 2 * width), jnp.float32),
        input_output_aliases=aliases,
        compiler_params=pltpu.CompilerParams(vmem_limit_bytes=40 * 2**20),
        cost_estimate=cost(heads, rows, rows),
    )(flags, *operands)


def rest_kernel(shards, meta_ref, q_ref, part_ref, kn_ref, vn_ref, *rest):
    text_refs = rest[:shards]
    o_ref, key_ref, val_ref, s_ref, p_ref = rest[-5:]
    near = kn_ref.shape[0]
    heads = val_ref.shape[0]
    ones_once(val_ref)
    for u in range(heads):
        cols = head_cols(u)
        key_ref[u, :near, :] = kn_ref[:, cols]
        val_ref[u, :near, :HEAD_DIM] = vn_ref[:, cols]
        at = near
        for text_ref in text_refs:
            rows = slice(at, at + text_ref.shape[1])
            key_ref[u, rows, :] = text_ref[0, :, cols]
            val_ref[u, rows, :HEAD_DIM] = text_ref[1, :, cols]
            at += text_ref.shape[1]

    def floor_of(u, rows):
        return part_ref[rows, head_cols(2 * u + 1)]

    def finish(u, rows, sums, largest):
        kept = jnp.exp2(floor_of(u, rows) - largest)
        summed = sums[:, :HEAD_DIM] + kept * part_ref[rows, head_cols(2 * u)]
        o_ref[rows, head_cols(u)] = (summed / (sums[:, HEAD_DIM:] + kept)).astype(jnp.bfloat16)

    near_tiles = near // TILE
    attend_blocks(
        heads,
        FRAME_TILES,
        lambda u, rows: q_ref[rows, head_cols(u)],
        lambda u: key_ref[u],
        [bias_of(meta_ref, 2 + i * near_tiles, near_tiles) for i in range(FRAME_TILES)],
        val_ref,
        s_ref,
        p_ref,
        floor_of,
        finish,
    )


def attend_rest(meta, q_hat, part, near_k, near_v, shards, first, heads, out=None):
    rows, width = q_hat.shape
    total = FRAME + TXT
    step = 1 if heads % 2 or first % 2 else 2
    wide = step * HEAD_DIM
    frame_block = pl.BlockSpec((FRAME, wide), lambda h, meta: (meta[0], first // step + h))
    in_specs = [
        frame_block,
        pl.BlockSpec((FRAME, 2 * wide), lambda h, meta: (meta[0], first // step + h)),
        pl.BlockSpec((None, FRAME, wide), lambda h, meta: (0, 0, h)),
        pl.BlockSpec((None, FRAME, wide), lambda h, meta: (near_v.shape[0] - 1, 0, h)),
    ] + [
        pl.BlockSpec(
            (2, None, shard.shape[2], wide), lambda h, meta: (0, meta[1], 0, first // step + h)
        )
        for shard in shards
    ]
    operands = [q_hat, part, near_k, near_v, *shards]
    aliases = {}
    if out is not None:
        in_specs.append(pl.BlockSpec(memory_space=pl.ANY))
        operands.append(out)
        aliases = {len(operands): 0}
    return pl.pallas_call(
        functools.partial(rest_kernel, len(shards)),
        grid_spec=pltpu.PrefetchScalarGridSpec(
            num_scalar_prefetch=1,
            grid=(heads // step,),
            in_specs=in_specs,
            out_specs=frame_block,
            scratch_shapes=[
                pltpu.VMEM((step, total, HEAD_DIM), jnp.bfloat16),
                pltpu.VMEM((step, total, 2 * HEAD_DIM), jnp.bfloat16),
                pltpu.VMEM((step, FRAME, total), jnp.float32),
                pltpu.VMEM((step, FRAME, total), jnp.bfloat16),
            ],
        ),
        out_shape=jax.ShapeDtypeStruct((rows, width), jnp.bfloat16),
        input_output_aliases=aliases,
        compiler_params=pltpu.CompilerParams(vmem_limit_bytes=32 * 2**20),
        cost_estimate=cost(heads, FRAME, total),
    )(meta, *operands)


def side_route(count, level):
    last = count // 2 - 1
    first, second, is_straight = [], [], [False] * count
    for k in range(last):
        low, high = 2 * k + 1, 2 * k + 2
        for source, target, relays in ((low, high, k < level), (high, low, k >= last - level)):
            if relays:
                first.append((source, source ^ 1))
                second.append((source ^ 1, target))
            else:
                first.append((source, target))
                is_straight[target] = True
    return first, second, is_straight


def after(value, *others):
    return lax.optimization_barrier((value, *others))[0]


def local(
    queries, keys, values, query_gain, key_gain, shapes, windows, text_keys, text_values, owner
):
    rows, width = queries.shape
    heads = width // HEAD_DIM
    count = lax.axis_size("seq")
    me = lax.axis_index("seq")
    odd = me % 2
    pair = [(i, i ^ 1) for i in range(count)]
    pair_frame, side_frame = 1 - odd, odd

    chosen = choose(owner, text_keys, text_values)
    both = jnp.concatenate([chosen, lax.ppermute(chosen, "seq", pair)], axis=2)
    pair_values = lax.dynamic_slice_in_dim(after(values, chosen), pair_frame * FRAME, FRAME, 0)
    near_values = lax.ppermute(pair_values[None], "seq", pair)
    if count <= 8:
        shards = [both] + [
            lax.ppermute(both, "seq", [(i, (i + 2 * k) % count) for i in range(count)])
            for k in range(1, count // 2)
        ]
    else:
        groups = [list(range(start, count, 2)) for start in range(2)]
        shards = [lax.all_gather(both, "seq", axis=2, tiled=True, axis_index_groups=groups)]

    place, own_flags, pair_meta, side_meta = plan(me, shapes, windows)
    query_wide, key_wide, _ = lax.optimization_barrier((queries, keys, chosen))
    query_wide = query_wide.astype(jnp.float32)
    key_wide = key_wide.astype(jnp.float32)
    squares = head_sum(
        jnp.stack([jnp.sum(query_wide * query_wide, axis=1), jnp.sum(key_wide * key_wide, axis=1)])
    )
    q_hat, k_hat = turn(place, squares, queries, keys, query_gain, key_gain)
    pair_keys = lax.dynamic_slice_in_dim(k_hat, pair_frame * FRAME, FRAME, 0)[None]
    near_keys = lax.ppermute(pair_keys, "seq", pair)
    part = attend_own(own_flags, q_hat, k_hat, values, 0, heads)
    out = attend_rest(pair_meta, q_hat, part, near_keys, near_values, shards, 0, heads)

    few = max(1, heads * 2 // 5)
    relays = count // 2 - 1 if count == 8 else 0
    parcels = (
        (few, relays, (near_values,)),
        (heads - few, 0, (near_keys, part, *shards)),
    )
    side_keys = lax.dynamic_slice_in_dim(k_hat, side_frame * FRAME, FRAME, 0)
    side_values = lax.dynamic_slice_in_dim(values, side_frame * FRAME, FRAME, 0)
    side_parcels = []
    start = 0
    for step, level, gate in parcels:
        cols = slice(start * HEAD_DIM, (start + step) * HEAD_DIM)
        parcel = jnp.stack([side_keys[:, cols], side_values[:, cols]])
        straight, relayed, is_straight = side_route(count, level)
        arrived = lax.ppermute(after(parcel, *gate), "seq", straight)
        if relayed:
            forwarded = lax.ppermute(arrived, "seq", relayed)
            if any(is_straight):
                forwarded = jnp.where(jnp.asarray(is_straight)[me], arrived, forwarded)
            arrived = forwarded
        side_parcels.append(arrived)
        start += step
    start = 0
    for (step, *_), parcel in zip(parcels, side_parcels):
        out = attend_rest(side_meta, q_hat, part, parcel, parcel, shards, start, step, out)
        start += step
    return out


def solution(mesh):
    placed = (
        P("seq", "head"),
        P("seq", "head"),
        P("seq", "head"),
        P("head"),
        P("head"),
        P(),
        P("seq", None),
        P(None, "seq", "head"),
        P(None, "seq", "head"),
        P(),
    )
    return jax.shard_map(
        local, mesh=mesh, in_specs=placed, out_specs=P("seq", "head"), check_vma=False
    )
```

time: 183 us -> 136 us (0.74)
  waiting for transfers between devices: 62.9 us -> 47.8 us
  other arithmetic: 16.5 us -> 4.93 us
  local copies, waits for them, and re-layouts: 23.2 us -> 13.6 us
  starting transfers between devices: 26.1 us -> 18.3 us
  Pallas kernels: 52.1 us -> 50.2 us
    ppermute x3, waiting for transfers between devices: 42.5 us -> 26.3 us  [local(): lax.ppermute(both, 'seq', [(i, (i + 2 * k) % count) for i in range(count)])]
    ppermute x6 -> x4, waiting for transfers between devices: 8.85 us -> 21.5 us  [the longest x1 8.41 us: local(): forwarded = lax.ppermute(arrived, 'seq', relayed)]
    ppermute x1, waiting for transfers between devices: 11.4 us -> 0.01 us  [local(): both = jnp.concatenate([chosen, lax.ppermute(chosen, 'seq', pair)], axis=2)]
    ppermute x6 -> x4, starting transfers between devices: 17.7 us -> 8.91 us  [the longest x2 4.34 us: local(): arrived = lax.ppermute(after(parcel, *gate), 'seq', straight)]
    gather x4 -> x0, local copies, waits for them, and re-layouts: 8.19 us -> none  [the longest x1 4.02 us: local(): text = jnp.take(text, slots, axis=1)]
    another operation x5 -> x2, other arithmetic: 4.29 us -> 0.24 us  [local(): parcel = jnp.stack([side_keys[:, cols], side_values[:, cols]])]
    mul x3 -> x0, other arithmetic: 2.42 us -> none  [the longest x1 2.04 us: local(): k_hat = turn(keys, cosine * key_scale, sine * key_scale, key_gain)]
    select_n x7 -> x0, other arithmetic: 2.22 us -> none  [the longest x2 2.04 us: local(): text = jnp.take(text, slots, axis=1)]
  transfers between devices with their start and end apart: 13 -> 11, of which waited for: 6 -> 7; matrix products, arithmetic and copies ran while one was open for 18% -> 9% of each run, Pallas kernels for 26% -> 31%
where the time goes in v2:
time: 136 us; the launch traced here: 135 us
  Pallas kernels  50.2 us (37%)
  waiting for transfers between devices  47.8 us (35%)
  starting transfers between devices  18.3 us (13%)
  local copies, waits for them, and re-layouts  13.6 us (10%)
  other arithmetic  4.93 us (4%)
    ppermute x3, waiting for transfers between devices, local(): lax.ppermute(both, 'seq', [(i, (i + 2 * k) % count) for i in range(count)])  26.3 us
    pallas_call x3, Pallas kernels, attend_rest(): pl.pallas_call(functools.partial(rest_kernel, len(shards)), grid_spec=plt...  21 us
    pallas_call x1, Pallas kernels, attend_own(): pl.pallas_call(own_kernel, grid_spec=pltpu.PrefetchScalarGridSpec(num_sca...  18.8 us
    ppermute x1, waiting for transfers between devices, local(): forwarded = lax.ppermute(arrived, 'seq', relayed)  8.41 us
    ppermute x1, waiting for transfers between devices, local(): near_values = lax.ppermute(pair_values[None], 'seq', pair)  7.09 us
    pallas_call x1, Pallas kernels, turn(): pl.pallas_call(turn_kernel, grid_spec=pltpu.PrefetchScalarGridSpec(num_sc...  6.49 us
    unnamed x32, local copies, waits for them, and re-layouts  6.46 us
    ppermute x2, waiting for transfers between devices, local(): arrived = lax.ppermute(after(parcel, *gate), 'seq', straight)  5.97 us
  transfers between devices with their start and end apart: 11, of which 7 were waited for; matrix products, arithmetic and copies ran while one was open for 9% of the time, Pallas kernels for 31%

profile of v2, /device:TPU:8, one launch (start us, length us, event | category | flops | bytes accessed | tf_op | source)
XLA Modules:
  0.0 135.1 jit_solution(17170050004399180261)
XLA Ops:
  0.0 2.4 %shard_map.128 = bf16[2,2,32,1280]{3,2,1,0:T(8,128)(2,1)} custom-call(s32[2]{0:T(128)} %owner_ref.1, bf16[8,32,1280]{2,1,0:T(8,128)(2,1)} %keys_ref.1, bf16[8,32,1280]{2,1,0:T(8,128)(2,1)} %values_ref.1), custom_call_target="tpu_custom_call" | custom-call | flops 1000 | bytes 1000 | tf_op jit(solution)/shard_map/pallas_call | solution.py:215
  2.4 1.5 %collective-permute-start.3 = (bf16[2,2,32,1280]{3,2,1,0:T(8,128)(2,1)}, bf16[2,2,32,1280]{3,2,1,0:T(8,128)(2,1)}, u32[]{:S(2)}, u32[]{:S(2)}) collective-permute-start(bf16[2,2,32,1280]{3,2,1,0:T(8,128)(2,1)} %shard_map.128), channel_id=1, source_target_pairs={{0,4},{4,0},{8,12},{12,8},{16,20},{20,16},{24,28},{28,24},{1,5},{5... | collective-permute-start | bytes 983048 | tf_op jit(solution)/shard_map/ppermute | solution.py:463
  3.9 3.6 %multiply_reduce_fusion = (f32[1024]{0:T(1024)S(1)}, f32[1024]{0:T(1024)S(1)}) fusion(bf16[1024,1280]{1,0:T(8,128)(2,1)} %refs_1_.1, bf16[1024,1280]{1,0:T(8,128)(2,1)} %refs_0_.1), kind=kLoop, calls=%fused_computation | loop fusion | flops 7862272 | bytes 5251072 | tf_op jit(solution)/shard_map/reduce_sum | solution.py:480
  7.5 0.1 collective-permute-start
  7.6 0.0 copy-start.15
  7.6 0.0 copy-start.14
  7.6 0.0 copy-start.12
  7.7 0.0 copy-start.13
  7.7 0.0 copy-start.1
  7.7 0.0 copy-start.5
  7.7 0.0 copy-start.6
  7.7 2.6 %dynamic-slice_bitcast_fusion = bf16[1,512,1280]{2,1,0:T(8,128)(2,1)} fusion(bf16[1024,1280]{1,0:T(8,128)(2,1)} %v_ref.1, s32[]{:T(128)S(6)} %select_n.17), kind=kLoop, calls=%fused_computation.3 | loop fusion | bytes 2621444 | tf_op jit(solution)/shard_map/broadcast_in_dim | solution.py:465
  10.3 0.5 collective-permute-start.8
  10.8 1.2 dynamic-slice_bitcast_fusion.2
  12.1 1.6 %collective-permute-start.1 = (f32[2,1024]{1,0:T(2,128)S(1)}, f32[2,1024]{1,0:T(2,128)S(1)}, u32[]{:S(2)}, u32[]{:S(2)}) collective-permute-start(f32[2,1024]{1,0:T(2,128)S(1)} %fusion), channel_id=1, source_target_pairs={{0,2},{1,3},{2,0},{3,1},{4,6},{5,7},{6,4},{7,5},{8,10},{9,11},{10,... | collective-permute-start | bytes 24584 | tf_op jit(solution)/shard_map/ppermute | solution.py:125
  13.7 1.9 %dynamic-slice_bitcast_fusion.4 = bf16[1,512,512]{2,1,0:T(8,128)(2,1)} fusion(bf16[1024,1280]{1,0:T(8,128)(2,1)} %v_ref.1, s32[]{:T(128)S(6)} %select_n.16), kind=kLoop, calls=%fused_computation.9 | loop fusion | bytes 1048580 | tf_op jit(solution)/shard_map/stack | solution.py:500
  15.5 0.6 reshape.16.shapes_ref
  16.1 0.7 reshape.17.windows_ref
  16.8 1.5 %shard_map.127 = (s32[24]{0:T(128)}, s32[64]{0:T(128)}, s32[18]{0:T(128)}, s32[18]{0:T(128)}) custom-call(s32[1]{0:T(128)} %bitcast.me_ref, s32[6]{0:T(128)} %reshape.16.shapes_ref, s32[216]{0:T(256)} %reshape.17.windows_ref), custom_call_target="tpu_custom_call" | custom-call | flops 1000 | bytes 1000 | tf_op jit(solution)/shard_map/pallas_call | solution.py:110
  18.4 0.0 copy-start.2
  18.4 1.7 %copy-done.2 = bf16[1024,1280]{1,0:T(8,128)(2,1)S(1)} copy-done((bf16[1024,1280]{1,0:T(8,128)(2,1)S(1)}, bf16[1024,1280]{1,0:T(8,128)(2,1)}, u32[]{:S(2)}) %copy-start.2) | copy-done | bytes 2621464
  20.1 0.7 copy-done.8
  20.8 6.5 %shard_map.129 = (bf16[1024,1280]{1,0:T(8,128)(2,1)S(1)}, bf16[1024,1280]{1,0:T(8,128)(2,1)S(1)}) custom-call(s32[24]{0:T(128)S(1)} %copy-done.8, s32[1,128]{1,0:T(1,128)S(1)} %copy-done.5, f32[1,128]{1,0:T(1,128)S(1)} %copy-done.6, f32[2,1024]{1,0:T(2,128)S(1)} %fusion.1.squares_ref, bf16[1024,1280]{1,0:T(8,128)(2,1)S(1)} %copy-done.2, ...), custom_call_target="tpu_custom_call" | custom-call | flops 1000 | bytes 1000 | tf_op jit(solution)/shard_map/pallas_call | solution.py:182
  27.3 0.1 dynamic-slice_bitcast_fusion.3
  27.4 0.1 dynamic-slice_bitcast_fusion.1
  27.6 0.0 copy-start.3
  27.6 1.6 %collective-permute-start.2 = (bf16[1,512,1280]{2,1,0:T(8,128)(2,1)S(1)}, bf16[1,512,1280]{2,1,0:T(8,128)(2,1)S(1)}, u32[]{:S(2)}, u32[]{:S(2)}) collective-permute-start(bf16[1,512,1280]{2,1,0:T(8,128)(2,1)S(1)} %dynamic-slice_bitcast_fusion.1), channel_id=1, source_target_pairs={{0,4},{4,0},{8,12},{12,8},{16,20},{20,16},{24,28},{28,24},{1,5},{5... | collective-permute-start | bytes 3932168 | tf_op jit(solution)/shard_map/ppermute | solution.py:484
  29.1 0.1 pad_maximum_fusion
  29.3 0.1 pad_maximum_fusion.1
  29.4 1.0 pad_maximum_fusion.2.rest_0_
  30.5 1.6 %collective-permute-start.4 = (bf16[2,2,64,1280]{3,2,1,0:T(8,128)(2,1)S(1)}, bf16[2,2,64,1280]{3,2,1,0:T(8,128)(2,1)S(1)}, u32[]{:S(2)}, u32[]{:S(2)}) collective-permute-start(bf16[2,2,64,1280]{3,2,1,0:T(8,128)(2,1)S(1)} %pad_maximum_fusion.2.rest_0_), channel_id=1, source_target_pairs={{0,8},{4,12},{8,16},{12,20},{16,24},{20,28},{24,0},{28,4},{1,9},{5... | collective-permute-start | bytes 1966088 | tf_op jit(solution)/shard_map/ppermute | solution.py:468
  32.1 1.2 collective-permute-start.5
  33.3 1.8 %collective-permute-start.6 = (bf16[2,2,64,1280]{3,2,1,0:T(8,128)(2,1)S(1)}, bf16[2,2,64,1280]{3,2,1,0:T(8,128)(2,1)S(1)}, u32[]{:S(2)}, u32[]{:S(2)}) collective-permute-start(bf16[2,2,64,1280]{3,2,1,0:T(8,128)(2,1)S(1)} %pad_maximum_fusion.2.rest_0_), channel_id=1, source_target_pairs={{0,24},{4,28},{8,0},{12,4},{16,8},{20,12},{24,16},{28,20},{1,25},{... | collective-permute-start | bytes 1966088 | tf_op jit(solution)/shard_map/ppermute | solution.py:468
  35.1 7.1 %collective-permute-done.8.vn_ref = bf16[1,512,1280]{2,1,0:T(8,128)(2,1)} collective-permute-done((bf16[1,512,1280]{2,1,0:T(8,128)(2,1)}, bf16[1,512,1280]{2,1,0:T(8,128)(2,1)}, u32[]{:S(2)}, u32[]{:S(2)}) %collective-permute-start.8) | collective-permute-done | bytes 1310752 | tf_op jit(solution)/shard_map/ppermute | solution.py:465
  42.2 2.4 %collective-permute-start.9 = (bf16[2,512,512]{2,1,0:T(8,128)(2,1)S(1)}, bf16[2,512,512]{2,1,0:T(8,128)(2,1)S(1)}, u32[]{:S(2)}, u32[]{:S(2)}) collective-permute-start(bf16[2,512,512]{2,1,0:T(8,128)(2,1)S(1)} %pad_maximum_fusion.1), channel_id=1, source_target_pairs={{4,0},{8,12},{12,8},{16,20},{20,16},{24,28},{5,1},{9,13},{13,9},{1... | collective-permute-start | bytes 3145736 | tf_op jit(solution)/shard_map/ppermute | solution.py:502
  44.7 18.8 %shard_map.130.part_ref = f32[1024,2560]{1,0:T(8,128)} custom-call(s32[64]{0:T(128)S(1)} %copy-done.9, bf16[1024,1280]{1,0:T(8,128)(2,1)S(1)} %get-tuple-element.20.q_ref, bf16[1024,1280]{1,0:T(8,128)(2,1)S(1)} %get-tuple-element.22.k_ref, bf16[1024,1280]{1,0:T(8,128)(2,1)S(1)} %copy-done.3), custom_call_target="tpu_custom_call" | custom-call | flops 10737418240 | bytes 62914560 | tf_op jit(solution)/shard_map/pallas_call | solution.py:328
  63.4 11.9 %collective-permute-done.4.rest_1_ = bf16[2,2,64,1280]{3,2,1,0:T(8,128)(2,1)S(1)} collective-permute-done((bf16[2,2,64,1280]{3,2,1,0:T(8,128)(2,1)S(1)}, bf16[2,2,64,1280]{3,2,1,0:T(8,128)(2,1)S(1)}, u32[]{:S(2)}, u32[]{:S(2)}) %collective-permute-start.4) | collective-permute-done | bytes 655392 | tf_op jit(solution)/shard_map/ppermute | solution.py:468
  75.3 12.6 %collective-permute-done.5.rest_2_ = bf16[2,2,64,1280]{3,2,1,0:T(8,128)(2,1)S(1)} collective-permute-done((bf16[2,2,64,1280]{3,2,1,0:T(8,128)(2,1)S(1)}, bf16[2,2,64,1280]{3,2,1,0:T(8,128)(2,1)S(1)}, u32[]{:S(2)}, u32[]{:S(2)}) %collective-permute-start.5) | collective-permute-done | bytes 655392 | tf_op jit(solution)/shard_map/ppermute | solution.py:468
  88.0 1.8 %collective-permute-done.6.rest_3_ = bf16[2,2,64,1280]{3,2,1,0:T(8,128)(2,1)S(1)} collective-permute-done((bf16[2,2,64,1280]{3,2,1,0:T(8,128)(2,1)S(1)}, bf16[2,2,64,1280]{3,2,1,0:T(8,128)(2,1)S(1)}, u32[]{:S(2)}, u32[]{:S(2)}) %collective-permute-start.6) | collective-permute-done | bytes 655392 | tf_op jit(solution)/shard_map/ppermute | solution.py:468
  89.8 1.9 %collective-permute-start.7 = (bf16[2,512,768]{2,1,0:T(8,128)(2,1)S(1)}, bf16[2,512,768]{2,1,0:T(8,128)(2,1)S(1)}, u32[]{:S(2)}, u32[]{:S(2)}) collective-permute-start(bf16[2,512,768]{2,1,0:T(8,128)(2,1)S(1)} %pad_maximum_fusion), channel_id=1, source_target_pairs={{4,8},{8,4},{12,16},{16,12},{20,24},{24,20},{5,9},{9,5},{13,17},{1... | collective-permute-start | bytes 4718600 | tf_op jit(solution)/shard_map/ppermute | solution.py:502
  91.7 0.5 collective-permute-done.9
  92.2 4.0 %collective-permute-start.10 = (bf16[2,512,512]{2,1,0:T(8,128)(2,1)S(1)}, bf16[2,512,512]{2,1,0:T(8,128)(2,1)S(1)}, u32[]{:S(2)}, u32[]{:S(2)}) collective-permute-start(bf16[2,512,512]{2,1,0:T(8,128)(2,1)S(1)} %collective-permute-done.9), channel_id=1, source_target_pairs={{0,8},{12,4},{8,16},{20,12},{16,24},{28,20},{1,9},{13,5},{9,17},{2... | collective-permute-start | bytes 3145736 | tf_op jit(solution)/shard_map/ppermute | solution.py:504
  96.3 4.0 %copy-done = f32[1024,2560]{1,0:T(8,128)S(1)} copy-done((f32[1024,2560]{1,0:T(8,128)S(1)}, f32[1024,2560]{1,0:T(8,128)}, u32[]{:S(2)}) %copy-start) | copy-done | bytes 10485784
  100.2 10.2 %shard_map.131.rest_4_ = bf16[1024,1280]{1,0:T(8,128)(2,1)} custom-call(s32[18]{0:T(128)S(1)} %copy-done.7, bf16[1024,1280]{1,0:T(8,128)(2,1)S(1)} %get-tuple-element.20.q_ref, f32[1024,2560]{1,0:T(8,128)S(1)} %copy-done, bf16[1,512,1280]{2,1,0:T(8,128)(2,1)S(1)} %collective-permute-done.2.kn_ref, bf16[1,512,1280]{2,1,0:T(8,128)(2,1)} %collective-permute-done.8.vn_ref, ...), custom_call_target="tpu_custom_call" | custom-call | flops 4026531840 | bytes 23592960 | tf_op jit(solution)/shard_map/pallas_call | solution.py:411
  110.4 8.4 %collective-permute-done.10.kn_ref.vn_ref = bf16[2,512,512]{2,1,0:T(8,128)(2,1)S(1)} collective-permute-done((bf16[2,512,512]{2,1,0:T(8,128)(2,1)S(1)}, bf16[2,512,512]{2,1,0:T(8,128)(2,1)S(1)}, u32[]{:S(2)}, u32[]{:S(2)}) %collective-permute-start.10) | collective-permute-done | bytes 1048608 | tf_op jit(solution)/shard_map/ppermute | solution.py:504
  118.8 4.6 %shard_map.132.rest_4_ = bf16[1024,1280]{1,0:T(8,128)(2,1)} custom-call(s32[18]{0:T(128)S(1)} %copy-done.4, bf16[1024,1280]{1,0:T(8,128)(2,1)S(1)} %get-tuple-element.20.q_ref, f32[1024,2560]{1,0:T(8,128)S(1)} %copy-done, bf16[2,512,512]{2,1,0:T(8,128)(2,1)S(1)} %collective-permute-done.10.kn_ref.vn_ref, ...), custom_call_target="tpu_custom_call", output_to_operand_aliasing={{}: (9, {})} | custom-call | flops 1610612736 | bytes 9437184 | tf_op jit(solution)/shard_map/pallas_call | solution.py:411
  123.4 5.5 %collective-permute-done.7.kn_ref.vn_ref = bf16[2,512,768]{2,1,0:T(8,128)(2,1)S(1)} collective-permute-done((bf16[2,512,768]{2,1,0:T(8,128)(2,1)S(1)}, bf16[2,512,768]{2,1,0:T(8,128)(2,1)S(1)}, u32[]{:S(2)}, u32[]{:S(2)}) %collective-permute-start.7) | collective-permute-done | bytes 1572896 | tf_op jit(solution)/shard_map/ppermute | solution.py:502
  128.9 6.3 %shard_map.133 = bf16[1024,1280]{1,0:T(8,128)(2,1)} custom-call(s32[18]{0:T(128)S(1)} %copy-done.4, bf16[1024,1280]{1,0:T(8,128)(2,1)S(1)} %get-tuple-element.20.q_ref, f32[1024,2560]{1,0:T(8,128)S(1)} %copy-done, bf16[2,512,768]{2,1,0:T(8,128)(2,1)S(1)} %collective-permute-done.7.kn_ref.vn_ref, ...), custom_call_target="tpu_custom_call", output_to_operand_aliasing={{}: (9, {})} | custom-call | flops 2415919104 | bytes 14155776 | tf_op jit(solution)/shard_map/pallas_call | solution.py:411
  (30 shorter events, 0.1 us)
Async XLA Ops:
  2.4 27.0 %collective-permute-start.3 = (bf16[2,2,32,1280]{3,2,1,0:T(8,128)(2,1)}, bf16[2,2,32,1280]{3,2,1,0:T(8,128)(2,1)}, u32[]{:S(2)}, u32[]{:S(2)}) collective-permute-start(bf16[2,2,32,1280]{3,2,1,0:T(8,128)(2,1)} %shard_map.128), channel_id=1, source_target_pairs={{0,4},{4,0},{8,12},{12,8},{16,20},{20,16},{24,28},{28,24},{1,5},{5... | collective-permute-start | bytes 983048 | tf_op jit(solution)/shard_map/ppermute | solution.py:463
  7.5 4.5 %collective-permute-start = (f32[2,1024]{1,0:T(2,128)S(1)}, f32[2,1024]{1,0:T(2,128)S(1)}, u32[]{:S(2)}, u32[]{:S(2)}) collective-permute-start(f32[2,1024]{1,0:T(2,128)S(1)} %pad_maximum_fusion.3), channel_id=1, source_target_pairs={{0,1},{1,0},{2,3},{3,2},{4,5},{5,4},{6,7},{7,6},{8,9},{9,8},{10,11... | collective-permute-start | bytes 24584 | tf_op jit(solution)/shard_map/ppermute | solution.py:125
  7.6 7.9 %copy-start.15 = (s32[2,3]{1,0:T(2,128)S(1)}, s32[2,3]{1,0:T(2,128)}, u32[]{:S(2)}) copy-start(s32[2,3]{1,0:T(2,128)} %param.18) | copy-start | bytes 76
  7.6 8.5 %copy-start.14 = (s32[8,27]{1,0:T(8,128)S(1)}, s32[8,27]{1,0:T(8,128)}, u32[]{:S(2)}) copy-start(s32[8,27]{1,0:T(8,128)} %param.19) | copy-start | bytes 2596
  7.6 10.6 %copy-start.12 = (f32[1280]{0:T(1024)S(1)}, f32[1280]{0:T(1024)}, u32[]{:S(2)}) copy-start(f32[1280]{0:T(1024)} %param.16) | copy-start | bytes 15364
  7.7 10.7 %copy-start.13 = (f32[1280]{0:T(1024)S(1)}, f32[1280]{0:T(1024)}, u32[]{:S(2)}) copy-start(f32[1280]{0:T(1024)} %param.17) | copy-start | bytes 15364
  7.7 10.7 %copy-start.1 = (bf16[1024,1280]{1,0:T(8,128)(2,1)S(1)}, bf16[1024,1280]{1,0:T(8,128)(2,1)}, u32[]{:S(2)}) copy-start(bf16[1024,1280]{1,0:T(8,128)(2,1)} %refs_1_.1) | copy-start | bytes 7864324
  7.7 10.7 %copy-start.5 = (s32[1,128]{1,0:T(1,128)S(1)}, s32[1,128]{1,0:T(1,128)}, u32[]{:S(2)}) copy-start(s32[1,128]{1,0:T(1,128)} %constant.39.part_ref) | copy-start | bytes 1540
  7.7 10.7 %copy-start.6 = (f32[1,128]{1,0:T(1,128)S(1)}, f32[1,128]{1,0:T(1,128)}, u32[]{:S(2)}) copy-start(f32[1,128]{1,0:T(1,128)} %constant.43.frequency_ref) | copy-start | bytes 1540
  10.3 31.9 %collective-permute-start.8 = (bf16[1,512,1280]{2,1,0:T(8,128)(2,1)}, bf16[1,512,1280]{2,1,0:T(8,128)(2,1)}, u32[]{:S(2)}, u32[]{:S(2)}) collective-permute-start(bf16[1,512,1280]{2,1,0:T(8,128)(2,1)} %dynamic-slice_bitcast_fusion), channel_id=1, source_target_pairs={{0,4},{4,0},{8,12},{12,8},{16,20},{20,16},{24,28},{28,24},{1,5},{5... | collective-permute-start | bytes 3932168 | tf_op jit(solution)/shard_map/ppermute | solution.py:465
  12.1 6.3 %collective-permute-start.1 = (f32[2,1024]{1,0:T(2,128)S(1)}, f32[2,1024]{1,0:T(2,128)S(1)}, u32[]{:S(2)}, u32[]{:S(2)}) collective-permute-start(f32[2,1024]{1,0:T(2,128)S(1)} %fusion), channel_id=1, source_target_pairs={{0,2},{1,3},{2,0},{3,1},{4,6},{5,7},{6,4},{7,5},{8,10},{9,11},{10,... | collective-permute-start | bytes 24584 | tf_op jit(solution)/shard_map/ppermute | solution.py:125
  18.4 1.7 %copy-start.2 = (bf16[1024,1280]{1,0:T(8,128)(2,1)S(1)}, bf16[1024,1280]{1,0:T(8,128)(2,1)}, u32[]{:S(2)}) copy-start(bf16[1024,1280]{1,0:T(8,128)(2,1)} %refs_0_.1) | copy-start | bytes 7864324
  20.1 0.7 copy-start.8
  27.5 1.8 %copy-start.10 = (bf16[1,512,512]{2,1,0:T(8,128)(2,1)S(1)}, bf16[1,512,512]{2,1,0:T(8,128)(2,1)}, u32[]{:S(2)}) copy-start(bf16[1,512,512]{2,1,0:T(8,128)(2,1)} %dynamic-slice_bitcast_fusion.4) | copy-start | bytes 1572868
  27.6 1.9 %copy-start.11 = (bf16[2,2,32,1280]{3,2,1,0:T(8,128)(2,1)S(1)}, bf16[2,2,32,1280]{3,2,1,0:T(8,128)(2,1)}, u32[]{:S(2)}) copy-start(bf16[2,2,32,1280]{3,2,1,0:T(8,128)(2,1)} %shard_map.128) | copy-start | bytes 983044
  27.6 17.1 %copy-start.3 = (bf16[1024,1280]{1,0:T(8,128)(2,1)S(1)}, bf16[1024,1280]{1,0:T(8,128)(2,1)}, u32[]{:S(2)}) copy-start(bf16[1024,1280]{1,0:T(8,128)(2,1)} %v_ref.1) | copy-start | bytes 7864324
  27.6 17.1 %copy-start.9 = (s32[64]{0:T(128)S(1)}, s32[64]{0:T(128)}, u32[]{:S(2)}) copy-start(s32[64]{0:T(128)} %get-tuple-element.21.meta_ref) | copy-start | bytes 772
  27.6 62.2 %collective-permute-start.2 = (bf16[1,512,1280]{2,1,0:T(8,128)(2,1)S(1)}, bf16[1,512,1280]{2,1,0:T(8,128)(2,1)S(1)}, u32[]{:S(2)}, u32[]{:S(2)}) collective-permute-start(bf16[1,512,1280]{2,1,0:T(8,128)(2,1)S(1)} %dynamic-slice_bitcast_fusion.1), channel_id=1, source_target_pairs={{0,4},{4,0},{8,12},{12,8},{16,20},{20,16},{24,28},{28,24},{1,5},{5... | collective-permute-start | bytes 3932168 | tf_op jit(solution)/shard_map/ppermute | solution.py:484
  30.5 44.9 %collective-permute-start.4 = (bf16[2,2,64,1280]{3,2,1,0:T(8,128)(2,1)S(1)}, bf16[2,2,64,1280]{3,2,1,0:T(8,128)(2,1)S(1)}, u32[]{:S(2)}, u32[]{:S(2)}) collective-permute-start(bf16[2,2,64,1280]{3,2,1,0:T(8,128)(2,1)S(1)} %pad_maximum_fusion.2.rest_0_), channel_id=1, source_target_pairs={{0,8},{4,12},{8,16},{12,20},{16,24},{20,28},{24,0},{28,4},{1,9},{5... | collective-permute-start | bytes 1966088 | tf_op jit(solution)/shard_map/ppermute | solution.py:468
  32.1 55.9 %collective-permute-start.5 = (bf16[2,2,64,1280]{3,2,1,0:T(8,128)(2,1)S(1)}, bf16[2,2,64,1280]{3,2,1,0:T(8,128)(2,1)S(1)}, u32[]{:S(2)}, u32[]{:S(2)}) collective-permute-start(bf16[2,2,64,1280]{3,2,1,0:T(8,128)(2,1)S(1)} %pad_maximum_fusion.2.rest_0_), channel_id=1, source_target_pairs={{0,16},{4,20},{8,24},{12,28},{16,0},{20,4},{24,8},{28,12},{1,17},{... | collective-permute-start | bytes 1966088 | tf_op jit(solution)/shard_map/ppermute | solution.py:468
  33.3 56.5 %collective-permute-start.6 = (bf16[2,2,64,1280]{3,2,1,0:T(8,128)(2,1)S(1)}, bf16[2,2,64,1280]{3,2,1,0:T(8,128)(2,1)S(1)}, u32[]{:S(2)}, u32[]{:S(2)}) collective-permute-start(bf16[2,2,64,1280]{3,2,1,0:T(8,128)(2,1)S(1)} %pad_maximum_fusion.2.rest_0_), channel_id=1, source_target_pairs={{0,24},{4,28},{8,0},{12,4},{16,8},{20,12},{24,16},{28,20},{1,25},{... | collective-permute-start | bytes 1966088 | tf_op jit(solution)/shard_map/ppermute | solution.py:468
  42.2 50.0 %collective-permute-start.9 = (bf16[2,512,512]{2,1,0:T(8,128)(2,1)S(1)}, bf16[2,512,512]{2,1,0:T(8,128)(2,1)S(1)}, u32[]{:S(2)}, u32[]{:S(2)}) collective-permute-start(bf16[2,512,512]{2,1,0:T(8,128)(2,1)S(1)} %pad_maximum_fusion.1), channel_id=1, source_target_pairs={{4,0},{8,12},{12,8},{16,20},{20,16},{24,28},{5,1},{9,13},{13,9},{1... | collective-permute-start | bytes 3145736 | tf_op jit(solution)/shard_map/ppermute | solution.py:502
  44.7 51.6 %copy-start.7 = (s32[18]{0:T(128)S(1)}, s32[18]{0:T(128)}, u32[]{:S(2)}) copy-start(s32[18]{0:T(128)} %get-tuple-element.26.meta_ref) | copy-start | bytes 220
  89.8 39.1 %collective-permute-start.7 = (bf16[2,512,768]{2,1,0:T(8,128)(2,1)S(1)}, bf16[2,512,768]{2,1,0:T(8,128)(2,1)S(1)}, u32[]{:S(2)}, u32[]{:S(2)}) collective-permute-start(bf16[2,512,768]{2,1,0:T(8,128)(2,1)S(1)} %pad_maximum_fusion), channel_id=1, source_target_pairs={{4,8},{8,4},{12,16},{16,12},{20,24},{24,20},{5,9},{9,5},{13,17},{1... | collective-permute-start | bytes 4718600 | tf_op jit(solution)/shard_map/ppermute | solution.py:502
  92.2 26.6 %collective-permute-start.10 = (bf16[2,512,512]{2,1,0:T(8,128)(2,1)S(1)}, bf16[2,512,512]{2,1,0:T(8,128)(2,1)S(1)}, u32[]{:S(2)}, u32[]{:S(2)}) collective-permute-start(bf16[2,512,512]{2,1,0:T(8,128)(2,1)S(1)} %collective-permute-done.9), channel_id=1, source_target_pairs={{0,8},{12,4},{8,16},{20,12},{16,24},{28,20},{1,9},{13,5},{9,17},{2... | collective-permute-start | bytes 3145736 | tf_op jit(solution)/shard_map/ppermute | solution.py:504
  96.3 4.0 %copy-start = (f32[1024,2560]{1,0:T(8,128)S(1)}, f32[1024,2560]{1,0:T(8,128)}, u32[]{:S(2)}) copy-start(f32[1024,2560]{1,0:T(8,128)} %shard_map.130.part_ref) | copy-start | bytes 31457284
  100.2 18.6 %copy-start.4 = (s32[18]{0:T(128)S(1)}, s32[18]{0:T(128)}, u32[]{:S(2)}) copy-start(s32[18]{0:T(128)} %get-tuple-element.16.meta_ref) | copy-start | bytes 220

commit v3 on v2

--- a/solution.py
+++ b/solution.py
@@ -262,10 +262,11 @@
 
     blocks = [(u, i) for i in range(tiles) for u in range(heads)]
     score(*blocks[0])
+    score(*blocks[1])
     waiting = None
     for at, block in enumerate(blocks):
-        if at + 1 < len(blocks):
-            score(*blocks[at + 1])
+        if at + 2 < len(blocks):
+            score(*blocks[at + 2])
         largest = weigh(*block)
         if waiting is not None:
             mix(*waiting)

time: 136 us -> 135 us (level)
  transfers between devices with their start and end apart: 11 -> 11, of which waited for: 7 -> 7; matrix products, arithmetic and copies ran while one was open for 9% -> 9% of each run, Pallas kernels for 31% -> 30%
where the time goes in v3:
time: 135 us
  Pallas kernels  49.3 us (37%)
  waiting for transfers between devices  48.5 us (36%)
  starting transfers between devices  18.3 us (14%)
  local copies, waits for them, and re-layouts  13.6 us (10%)
  other arithmetic  4.93 us (4%)
    ppermute x3, waiting for transfers between devices, local(): lax.ppermute(both, 'seq', [(i, (i + 2 * k) % count) for i in range(count)])  26.6 us
    pallas_call x3, Pallas kernels, attend_rest(): pl.pallas_call(functools.partial(rest_kernel, len(shards)), grid_spec=plt...  20.4 us
    pallas_call x1, Pallas kernels, attend_own(): pl.pallas_call(own_kernel, grid_spec=pltpu.PrefetchScalarGridSpec(num_sca...  18.5 us
    ppermute x1, waiting for transfers between devices, local(): forwarded = lax.ppermute(arrived, 'seq', relayed)  8.7 us
    ppermute x1, waiting for transfers between devices, local(): near_values = lax.ppermute(pair_values[None], 'seq', pair)  7.09 us
    pallas_call x1, Pallas kernels, turn(): pl.pallas_call(turn_kernel, grid_spec=pltpu.PrefetchScalarGridSpec(num_sc...  6.49 us
    unnamed x32, local copies, waits for them, and re-layouts  6.46 us
    ppermute x2, waiting for transfers between devices, local(): arrived = lax.ppermute(after(parcel, *gate), 'seq', straight)  6.09 us
  transfers between devices with their start and end apart: 11, of which 7 were waited for; matrix products, arithmetic and copies ran while one was open for 9% of the time, Pallas kernels for 30%

profile of v3, /device:TPU:8, one launch (start us, length us, event | category | flops | bytes accessed | tf_op | source)
XLA Modules:
  0.0 135.0 jit_solution(9105022806435005681)
XLA Ops:
  0.0 2.4 %shard_map.128 = bf16[2,2,32,1280]{3,2,1,0:T(8,128)(2,1)} custom-call(s32[2]{0:T(128)} %owner_ref.1, bf16[8,32,1280]{2,1,0:T(8,128)(2,1)} %keys_ref.1, bf16[8,32,1280]{2,1,0:T(8,128)(2,1)} %values_ref.1), custom_call_target="tpu_custom_call" | custom-call | flops 1000 | bytes 1000 | tf_op jit(solution)/shard_map/pallas_call | solution.py:215
  2.4 1.5 %collective-permute-start.3 = (bf16[2,2,32,1280]{3,2,1,0:T(8,128)(2,1)}, bf16[2,2,32,1280]{3,2,1,0:T(8,128)(2,1)}, u32[]{:S(2)}, u32[]{:S(2)}) collective-permute-start(bf16[2,2,32,1280]{3,2,1,0:T(8,128)(2,1)} %shard_map.128), channel_id=1, source_target_pairs={{0,4},{4,0},{8,12},{12,8},{16,20},{20,16},{24,28},{28,24},{1,5},{5... | collective-permute-start | bytes 983048 | tf_op jit(solution)/shard_map/ppermute | solution.py:464
  3.9 3.6 %multiply_reduce_fusion = (f32[1024]{0:T(1024)S(1)}, f32[1024]{0:T(1024)S(1)}) fusion(bf16[1024,1280]{1,0:T(8,128)(2,1)} %refs_1_.1, bf16[1024,1280]{1,0:T(8,128)(2,1)} %refs_0_.1), kind=kLoop, calls=%fused_computation | loop fusion | flops 7862272 | bytes 5251072 | tf_op jit(solution)/shard_map/reduce_sum | solution.py:481
  7.5 0.1 collective-permute-start
  7.6 0.0 copy-start.15
  7.6 0.0 copy-start.14
  7.6 0.0 copy-start.12
  7.7 0.0 copy-start.13
  7.7 0.0 copy-start.1
  7.7 0.0 copy-start.5
  7.7 0.0 copy-start.6
  7.7 2.6 %dynamic-slice_bitcast_fusion = bf16[1,512,1280]{2,1,0:T(8,128)(2,1)} fusion(bf16[1024,1280]{1,0:T(8,128)(2,1)} %v_ref.1, s32[]{:T(128)S(6)} %select_n.17), kind=kLoop, calls=%fused_computation.3 | loop fusion | bytes 2621444 | tf_op jit(solution)/shard_map/broadcast_in_dim | solution.py:466
  10.3 0.5 collective-permute-start.8
  10.8 1.2 dynamic-slice_bitcast_fusion.2
  12.1 1.6 %collective-permute-start.1 = (f32[2,1024]{1,0:T(2,128)S(1)}, f32[2,1024]{1,0:T(2,128)S(1)}, u32[]{:S(2)}, u32[]{:S(2)}) collective-permute-start(f32[2,1024]{1,0:T(2,128)S(1)} %fusion), channel_id=1, source_target_pairs={{0,2},{1,3},{2,0},{3,1},{4,6},{5,7},{6,4},{7,5},{8,10},{9,11},{10,... | collective-permute-start | bytes 24584 | tf_op jit(solution)/shard_map/ppermute | solution.py:125
  13.7 1.9 %dynamic-slice_bitcast_fusion.4 = bf16[1,512,512]{2,1,0:T(8,128)(2,1)} fusion(bf16[1024,1280]{1,0:T(8,128)(2,1)} %v_ref.1, s32[]{:T(128)S(6)} %select_n.16), kind=kLoop, calls=%fused_computation.9 | loop fusion | bytes 1048580 | tf_op jit(solution)/shard_map/stack | solution.py:501
  15.5 0.6 reshape.16.shapes_ref
  16.1 0.7 reshape.17.windows_ref
  16.8 1.5 %shard_map.127 = (s32[24]{0:T(128)}, s32[64]{0:T(128)}, s32[18]{0:T(128)}, s32[18]{0:T(128)}) custom-call(s32[1]{0:T(128)} %bitcast.me_ref, s32[6]{0:T(128)} %reshape.16.shapes_ref, s32[216]{0:T(256)} %reshape.17.windows_ref), custom_call_target="tpu_custom_call" | custom-call | flops 1000 | bytes 1000 | tf_op jit(solution)/shard_map/pallas_call | solution.py:110
  18.4 0.0 copy-start.2
  18.4 1.7 %copy-done.2 = bf16[1024,1280]{1,0:T(8,128)(2,1)S(1)} copy-done((bf16[1024,1280]{1,0:T(8,128)(2,1)S(1)}, bf16[1024,1280]{1,0:T(8,128)(2,1)}, u32[]{:S(2)}) %copy-start.2) | copy-done | bytes 2621464
  20.1 0.7 copy-done.8
  20.8 6.5 %shard_map.129 = (bf16[1024,1280]{1,0:T(8,128)(2,1)S(1)}, bf16[1024,1280]{1,0:T(8,128)(2,1)S(1)}) custom-call(s32[24]{0:T(128)S(1)} %copy-done.8, s32[1,128]{1,0:T(1,128)S(1)} %copy-done.5, f32[1,128]{1,0:T(1,128)S(1)} %copy-done.6, f32[2,1024]{1,0:T(2,128)S(1)} %fusion.1.squares_ref, bf16[1024,1280]{1,0:T(8,128)(2,1)S(1)} %copy-done.2, ...), custom_call_target="tpu_custom_call" | custom-call | flops 1000 | bytes 1000 | tf_op jit(solution)/shard_map/pallas_call | solution.py:182
  27.3 0.1 dynamic-slice_bitcast_fusion.3
  27.4 0.1 dynamic-slice_bitcast_fusion.1
  27.6 0.0 copy-start.3
  27.6 1.6 %collective-permute-start.2 = (bf16[1,512,1280]{2,1,0:T(8,128)(2,1)S(1)}, bf16[1,512,1280]{2,1,0:T(8,128)(2,1)S(1)}, u32[]{:S(2)}, u32[]{:S(2)}) collective-permute-start(bf16[1,512,1280]{2,1,0:T(8,128)(2,1)S(1)} %dynamic-slice_bitcast_fusion.1), channel_id=1, source_target_pairs={{0,4},{4,0},{8,12},{12,8},{16,20},{20,16},{24,28},{28,24},{1,5},{5... | collective-permute-start | bytes 3932168 | tf_op jit(solution)/shard_map/ppermute | solution.py:485
  29.1 0.1 pad_maximum_fusion
  29.3 0.1 pad_maximum_fusion.1
  29.4 1.0 pad_maximum_fusion.2.rest_0_
  30.5 1.6 %collective-permute-start.4 = (bf16[2,2,64,1280]{3,2,1,0:T(8,128)(2,1)S(1)}, bf16[2,2,64,1280]{3,2,1,0:T(8,128)(2,1)S(1)}, u32[]{:S(2)}, u32[]{:S(2)}) collective-permute-start(bf16[2,2,64,1280]{3,2,1,0:T(8,128)(2,1)S(1)} %pad_maximum_fusion.2.rest_0_), channel_id=1, source_target_pairs={{0,8},{4,12},{8,16},{12,20},{16,24},{20,28},{24,0},{28,4},{1,9},{5... | collective-permute-start | bytes 1966088 | tf_op jit(solution)/shard_map/ppermute | solution.py:469
  32.1 1.2 collective-permute-start.5
  33.3 1.8 %collective-permute-start.6 = (bf16[2,2,64,1280]{3,2,1,0:T(8,128)(2,1)S(1)}, bf16[2,2,64,1280]{3,2,1,0:T(8,128)(2,1)S(1)}, u32[]{:S(2)}, u32[]{:S(2)}) collective-permute-start(bf16[2,2,64,1280]{3,2,1,0:T(8,128)(2,1)S(1)} %pad_maximum_fusion.2.rest_0_), channel_id=1, source_target_pairs={{0,24},{4,28},{8,0},{12,4},{16,8},{20,12},{24,16},{28,20},{1,25},{... | collective-permute-start | bytes 1966088 | tf_op jit(solution)/shard_map/ppermute | solution.py:469
  35.1 7.1 %collective-permute-done.8.vn_ref = bf16[1,512,1280]{2,1,0:T(8,128)(2,1)} collective-permute-done((bf16[1,512,1280]{2,1,0:T(8,128)(2,1)}, bf16[1,512,1280]{2,1,0:T(8,128)(2,1)}, u32[]{:S(2)}, u32[]{:S(2)}) %collective-permute-start.8) | collective-permute-done | bytes 1310752 | tf_op jit(solution)/shard_map/ppermute | solution.py:466
  42.2 2.4 %collective-permute-start.9 = (bf16[2,512,512]{2,1,0:T(8,128)(2,1)S(1)}, bf16[2,512,512]{2,1,0:T(8,128)(2,1)S(1)}, u32[]{:S(2)}, u32[]{:S(2)}) collective-permute-start(bf16[2,512,512]{2,1,0:T(8,128)(2,1)S(1)} %pad_maximum_fusion.1), channel_id=1, source_target_pairs={{4,0},{8,12},{12,8},{16,20},{20,16},{24,28},{5,1},{9,13},{13,9},{1... | collective-permute-start | bytes 3145736 | tf_op jit(solution)/shard_map/ppermute | solution.py:503
  44.7 18.5 %shard_map.130.part_ref = f32[1024,2560]{1,0:T(8,128)} custom-call(s32[64]{0:T(128)S(1)} %copy-done.9, bf16[1024,1280]{1,0:T(8,128)(2,1)S(1)} %get-tuple-element.20.q_ref, bf16[1024,1280]{1,0:T(8,128)(2,1)S(1)} %get-tuple-element.22.k_ref, bf16[1024,1280]{1,0:T(8,128)(2,1)S(1)} %copy-done.3), custom_call_target="tpu_custom_call" | custom-call | flops 10737418240 | bytes 62914560 | tf_op jit(solution)/shard_map/pallas_call | solution.py:329
  63.2 12.1 %collective-permute-done.4.rest_1_ = bf16[2,2,64,1280]{3,2,1,0:T(8,128)(2,1)S(1)} collective-permute-done((bf16[2,2,64,1280]{3,2,1,0:T(8,128)(2,1)S(1)}, bf16[2,2,64,1280]{3,2,1,0:T(8,128)(2,1)S(1)}, u32[]{:S(2)}, u32[]{:S(2)}) %collective-permute-start.4) | collective-permute-done | bytes 655392 | tf_op jit(solution)/shard_map/ppermute | solution.py:469
  75.3 12.6 %collective-permute-done.5.rest_2_ = bf16[2,2,64,1280]{3,2,1,0:T(8,128)(2,1)S(1)} collective-permute-done((bf16[2,2,64,1280]{3,2,1,0:T(8,128)(2,1)S(1)}, bf16[2,2,64,1280]{3,2,1,0:T(8,128)(2,1)S(1)}, u32[]{:S(2)}, u32[]{:S(2)}) %collective-permute-start.5) | collective-permute-done | bytes 655392 | tf_op jit(solution)/shard_map/ppermute | solution.py:469
  88.0 1.8 %collective-permute-done.6.rest_3_ = bf16[2,2,64,1280]{3,2,1,0:T(8,128)(2,1)S(1)} collective-permute-done((bf16[2,2,64,1280]{3,2,1,0:T(8,128)(2,1)S(1)}, bf16[2,2,64,1280]{3,2,1,0:T(8,128)(2,1)S(1)}, u32[]{:S(2)}, u32[]{:S(2)}) %collective-permute-start.6) | collective-permute-done | bytes 655392 | tf_op jit(solution)/shard_map/ppermute | solution.py:469
  89.8 1.9 %collective-permute-start.7 = (bf16[2,512,768]{2,1,0:T(8,128)(2,1)S(1)}, bf16[2,512,768]{2,1,0:T(8,128)(2,1)S(1)}, u32[]{:S(2)}, u32[]{:S(2)}) collective-permute-start(bf16[2,512,768]{2,1,0:T(8,128)(2,1)S(1)} %pad_maximum_fusion), channel_id=1, source_target_pairs={{4,8},{8,4},{12,16},{16,12},{20,24},{24,20},{5,9},{9,5},{13,17},{1... | collective-permute-start | bytes 4718600 | tf_op jit(solution)/shard_map/ppermute | solution.py:503
  91.7 0.5 collective-permute-done.9
  92.2 4.0 %collective-permute-start.10 = (bf16[2,512,512]{2,1,0:T(8,128)(2,1)S(1)}, bf16[2,512,512]{2,1,0:T(8,128)(2,1)S(1)}, u32[]{:S(2)}, u32[]{:S(2)}) collective-permute-start(bf16[2,512,512]{2,1,0:T(8,128)(2,1)S(1)} %collective-permute-done.9), channel_id=1, source_target_pairs={{0,8},{12,4},{8,16},{20,12},{16,24},{28,20},{1,9},{13,5},{9,17},{2... | collective-permute-start | bytes 3145736 | tf_op jit(solution)/shard_map/ppermute | solution.py:505
  96.3 4.0 %copy-done = f32[1024,2560]{1,0:T(8,128)S(1)} copy-done((f32[1024,2560]{1,0:T(8,128)S(1)}, f32[1024,2560]{1,0:T(8,128)}, u32[]{:S(2)}) %copy-start) | copy-done | bytes 10485784
  100.2 9.9 %shard_map.131.rest_4_ = bf16[1024,1280]{1,0:T(8,128)(2,1)} custom-call(s32[18]{0:T(128)S(1)} %copy-done.7, bf16[1024,1280]{1,0:T(8,128)(2,1)S(1)} %get-tuple-element.20.q_ref, f32[1024,2560]{1,0:T(8,128)S(1)} %copy-done, bf16[1,512,1280]{2,1,0:T(8,128)(2,1)S(1)} %collective-permute-done.2.kn_ref, bf16[1,512,1280]{2,1,0:T(8,128)(2,1)} %collective-permute-done.8.vn_ref, ...), custom_call_target="tpu_custom_call" | custom-call | flops 4026531840 | bytes 23592960 | tf_op jit(solution)/shard_map/pallas_call | solution.py:412
  110.1 8.7 %collective-permute-done.10.kn_ref.vn_ref = bf16[2,512,512]{2,1,0:T(8,128)(2,1)S(1)} collective-permute-done((bf16[2,512,512]{2,1,0:T(8,128)(2,1)S(1)}, bf16[2,512,512]{2,1,0:T(8,128)(2,1)S(1)}, u32[]{:S(2)}, u32[]{:S(2)}) %collective-permute-start.10) | collective-permute-done | bytes 1048608 | tf_op jit(solution)/shard_map/ppermute | solution.py:505
  118.8 4.5 %shard_map.132.rest_4_ = bf16[1024,1280]{1,0:T(8,128)(2,1)} custom-call(s32[18]{0:T(128)S(1)} %copy-done.4, bf16[1024,1280]{1,0:T(8,128)(2,1)S(1)} %get-tuple-element.20.q_ref, f32[1024,2560]{1,0:T(8,128)S(1)} %copy-done, bf16[2,512,512]{2,1,0:T(8,128)(2,1)S(1)} %collective-permute-done.10.kn_ref.vn_ref, ...), custom_call_target="tpu_custom_call", output_to_operand_aliasing={{}: (9, {})} | custom-call | flops 1610612736 | bytes 9437184 | tf_op jit(solution)/shard_map/pallas_call | solution.py:412
  123.3 5.6 %collective-permute-done.7.kn_ref.vn_ref = bf16[2,512,768]{2,1,0:T(8,128)(2,1)S(1)} collective-permute-done((bf16[2,512,768]{2,1,0:T(8,128)(2,1)S(1)}, bf16[2,512,768]{2,1,0:T(8,128)(2,1)S(1)}, u32[]{:S(2)}, u32[]{:S(2)}) %collective-permute-start.7) | collective-permute-done | bytes 1572896 | tf_op jit(solution)/shard_map/ppermute | solution.py:503
  128.9 6.1 %shard_map.133 = bf16[1024,1280]{1,0:T(8,128)(2,1)} custom-call(s32[18]{0:T(128)S(1)} %copy-done.4, bf16[1024,1280]{1,0:T(8,128)(2,1)S(1)} %get-tuple-element.20.q_ref, f32[1024,2560]{1,0:T(8,128)S(1)} %copy-done, bf16[2,512,768]{2,1,0:T(8,128)(2,1)S(1)} %collective-permute-done.7.kn_ref.vn_ref, ...), custom_call_target="tpu_custom_call", output_to_operand_aliasing={{}: (9, {})} | custom-call | flops 2415919104 | bytes 14155776 | tf_op jit(solution)/shard_map/pallas_call | solution.py:412
  (30 shorter events, 0.1 us)
Async XLA Ops:
  2.4 27.0 %collective-permute-start.3 = (bf16[2,2,32,1280]{3,2,1,0:T(8,128)(2,1)}, bf16[2,2,32,1280]{3,2,1,0:T(8,128)(2,1)}, u32[]{:S(2)}, u32[]{:S(2)}) collective-permute-start(bf16[2,2,32,1280]{3,2,1,0:T(8,128)(2,1)} %shard_map.128), channel_id=1, source_target_pairs={{0,4},{4,0},{8,12},{12,8},{16,20},{20,16},{24,28},{28,24},{1,5},{5... | collective-permute-start | bytes 983048 | tf_op jit(solution)/shard_map/ppermute | solution.py:464
  7.5 4.5 %collective-permute-start = (f32[2,1024]{1,0:T(2,128)S(1)}, f32[2,1024]{1,0:T(2,128)S(1)}, u32[]{:S(2)}, u32[]{:S(2)}) collective-permute-start(f32[2,1024]{1,0:T(2,128)S(1)} %pad_maximum_fusion.3), channel_id=1, source_target_pairs={{0,1},{1,0},{2,3},{3,2},{4,5},{5,4},{6,7},{7,6},{8,9},{9,8},{10,11... | collective-permute-start | bytes 24584 | tf_op jit(solution)/shard_map/ppermute | solution.py:125
  7.6 7.9 %copy-start.15 = (s32[2,3]{1,0:T(2,128)S(1)}, s32[2,3]{1,0:T(2,128)}, u32[]{:S(2)}) copy-start(s32[2,3]{1,0:T(2,128)} %param.18) | copy-start | bytes 76
  7.6 8.5 %copy-start.14 = (s32[8,27]{1,0:T(8,128)S(1)}, s32[8,27]{1,0:T(8,128)}, u32[]{:S(2)}) copy-start(s32[8,27]{1,0:T(8,128)} %param.19) | copy-start | bytes 2596
  7.6 10.6 %copy-start.12 = (f32[1280]{0:T(1024)S(1)}, f32[1280]{0:T(1024)}, u32[]{:S(2)}) copy-start(f32[1280]{0:T(1024)} %param.16) | copy-start | bytes 15364
  7.7 10.7 %copy-start.13 = (f32[1280]{0:T(1024)S(1)}, f32[1280]{0:T(1024)}, u32[]{:S(2)}) copy-start(f32[1280]{0:T(1024)} %param.17) | copy-start | bytes 15364
  7.7 10.7 %copy-start.1 = (bf16[1024,1280]{1,0:T(8,128)(2,1)S(1)}, bf16[1024,1280]{1,0:T(8,128)(2,1)}, u32[]{:S(2)}) copy-start(bf16[1024,1280]{1,0:T(8,128)(2,1)} %refs_1_.1) | copy-start | bytes 7864324
  7.7 10.7 %copy-start.5 = (s32[1,128]{1,0:T(1,128)S(1)}, s32[1,128]{1,0:T(1,128)}, u32[]{:S(2)}) copy-start(s32[1,128]{1,0:T(1,128)} %constant.39.part_ref) | copy-start | bytes 1540
  7.7 10.7 %copy-start.6 = (f32[1,128]{1,0:T(1,128)S(1)}, f32[1,128]{1,0:T(1,128)}, u32[]{:S(2)}) copy-start(f32[1,128]{1,0:T(1,128)} %constant.43.frequency_ref) | copy-start | bytes 1540
  10.3 31.9 %collective-permute-start.8 = (bf16[1,512,1280]{2,1,0:T(8,128)(2,1)}, bf16[1,512,1280]{2,1,0:T(8,128)(2,1)}, u32[]{:S(2)}, u32[]{:S(2)}) collective-permute-start(bf16[1,512,1280]{2,1,0:T(8,128)(2,1)} %dynamic-slice_bitcast_fusion), channel_id=1, source_target_pairs={{0,4},{4,0},{8,12},{12,8},{16,20},{20,16},{24,28},{28,24},{1,5},{5... | collective-permute-start | bytes 3932168 | tf_op jit(solution)/shard_map/ppermute | solution.py:466
  12.1 6.3 %collective-permute-start.1 = (f32[2,1024]{1,0:T(2,128)S(1)}, f32[2,1024]{1,0:T(2,128)S(1)}, u32[]{:S(2)}, u32[]{:S(2)}) collective-permute-start(f32[2,1024]{1,0:T(2,128)S(1)} %fusion), channel_id=1, source_target_pairs={{0,2},{1,3},{2,0},{3,1},{4,6},{5,7},{6,4},{7,5},{8,10},{9,11},{10,... | collective-permute-start | bytes 24584 | tf_op jit(solution)/shard_map/ppermute | solution.py:125
  18.4 1.7 %copy-start.2 = (bf16[1024,1280]{1,0:T(8,128)(2,1)S(1)}, bf16[1024,1280]{1,0:T(8,128)(2,1)}, u32[]{:S(2)}) copy-start(bf16[1024,1280]{1,0:T(8,128)(2,1)} %refs_0_.1) | copy-start | bytes 7864324
  20.1 0.7 copy-start.8
  27.5 1.8 %copy-start.10 = (bf16[1,512,512]{2,1,0:T(8,128)(2,1)S(1)}, bf16[1,512,512]{2,1,0:T(8,128)(2,1)}, u32[]{:S(2)}) copy-start(bf16[1,512,512]{2,1,0:T(8,128)(2,1)} %dynamic-slice_bitcast_fusion.4) | copy-start | bytes 1572868
  27.6 1.9 %copy-start.11 = (bf16[2,2,32,1280]{3,2,1,0:T(8,128)(2,1)S(1)}, bf16[2,2,32,1280]{3,2,1,0:T(8,128)(2,1)}, u32[]{:S(2)}) copy-start(bf16[2,2,32,1280]{3,2,1,0:T(8,128)(2,1)} %shard_map.128) | copy-start | bytes 983044
  27.6 17.1 %copy-start.3 = (bf16[1024,1280]{1,0:T(8,128)(2,1)S(1)}, bf16[1024,1280]{1,0:T(8,128)(2,1)}, u32[]{:S(2)}) copy-start(bf16[1024,1280]{1,0:T(8,128)(2,1)} %v_ref.1) | copy-start | bytes 7864324
  27.6 17.1 %copy-start.9 = (s32[64]{0:T(128)S(1)}, s32[64]{0:T(128)}, u32[]{:S(2)}) copy-start(s32[64]{0:T(128)} %get-tuple-element.21.meta_ref) | copy-start | bytes 772
  27.6 62.2 %collective-permute-start.2 = (bf16[1,512,1280]{2,1,0:T(8,128)(2,1)S(1)}, bf16[1,512,1280]{2,1,0:T(8,128)(2,1)S(1)}, u32[]{:S(2)}, u32[]{:S(2)}) collective-permute-start(bf16[1,512,1280]{2,1,0:T(8,128)(2,1)S(1)} %dynamic-slice_bitcast_fusion.1), channel_id=1, source_target_pairs={{0,4},{4,0},{8,12},{12,8},{16,20},{20,16},{24,28},{28,24},{1,5},{5... | collective-permute-start | bytes 3932168 | tf_op jit(solution)/shard_map/ppermute | solution.py:485
  30.5 44.9 %collective-permute-start.4 = (bf16[2,2,64,1280]{3,2,1,0:T(8,128)(2,1)S(1)}, bf16[2,2,64,1280]{3,2,1,0:T(8,128)(2,1)S(1)}, u32[]{:S(2)}, u32[]{:S(2)}) collective-permute-start(bf16[2,2,64,1280]{3,2,1,0:T(8,128)(2,1)S(1)} %pad_maximum_fusion.2.rest_0_), channel_id=1, source_target_pairs={{0,8},{4,12},{8,16},{12,20},{16,24},{20,28},{24,0},{28,4},{1,9},{5... | collective-permute-start | bytes 1966088 | tf_op jit(solution)/shard_map/ppermute | solution.py:469
  32.1 55.9 %collective-permute-start.5 = (bf16[2,2,64,1280]{3,2,1,0:T(8,128)(2,1)S(1)}, bf16[2,2,64,1280]{3,2,1,0:T(8,128)(2,1)S(1)}, u32[]{:S(2)}, u32[]{:S(2)}) collective-permute-start(bf16[2,2,64,1280]{3,2,1,0:T(8,128)(2,1)S(1)} %pad_maximum_fusion.2.rest_0_), channel_id=1, source_target_pairs={{0,16},{4,20},{8,24},{12,28},{16,0},{20,4},{24,8},{28,12},{1,17},{... | collective-permute-start | bytes 1966088 | tf_op jit(solution)/shard_map/ppermute | solution.py:469
  33.3 56.5 %collective-permute-start.6 = (bf16[2,2,64,1280]{3,2,1,0:T(8,128)(2,1)S(1)}, bf16[2,2,64,1280]{3,2,1,0:T(8,128)(2,1)S(1)}, u32[]{:S(2)}, u32[]{:S(2)}) collective-permute-start(bf16[2,2,64,1280]{3,2,1,0:T(8,128)(2,1)S(1)} %pad_maximum_fusion.2.rest_0_), channel_id=1, source_target_pairs={{0,24},{4,28},{8,0},{12,4},{16,8},{20,12},{24,16},{28,20},{1,25},{... | collective-permute-start | bytes 1966088 | tf_op jit(solution)/shard_map/ppermute | solution.py:469
  42.2 50.0 %collective-permute-start.9 = (bf16[2,512,512]{2,1,0:T(8,128)(2,1)S(1)}, bf16[2,512,512]{2,1,0:T(8,128)(2,1)S(1)}, u32[]{:S(2)}, u32[]{:S(2)}) collective-permute-start(bf16[2,512,512]{2,1,0:T(8,128)(2,1)S(1)} %pad_maximum_fusion.1), channel_id=1, source_target_pairs={{4,0},{8,12},{12,8},{16,20},{20,16},{24,28},{5,1},{9,13},{13,9},{1... | collective-permute-start | bytes 3145736 | tf_op jit(solution)/shard_map/ppermute | solution.py:503
  44.7 51.6 %copy-start.7 = (s32[18]{0:T(128)S(1)}, s32[18]{0:T(128)}, u32[]{:S(2)}) copy-start(s32[18]{0:T(128)} %get-tuple-element.26.meta_ref) | copy-start | bytes 220
  89.8 39.1 %collective-permute-start.7 = (bf16[2,512,768]{2,1,0:T(8,128)(2,1)S(1)}, bf16[2,512,768]{2,1,0:T(8,128)(2,1)S(1)}, u32[]{:S(2)}, u32[]{:S(2)}) collective-permute-start(bf16[2,512,768]{2,1,0:T(8,128)(2,1)S(1)} %pad_maximum_fusion), channel_id=1, source_target_pairs={{4,8},{8,4},{12,16},{16,12},{20,24},{24,20},{5,9},{9,5},{13,17},{1... | collective-permute-start | bytes 4718600 | tf_op jit(solution)/shard_map/ppermute | solution.py:503
  92.2 26.6 %collective-permute-start.10 = (bf16[2,512,512]{2,1,0:T(8,128)(2,1)S(1)}, bf16[2,512,512]{2,1,0:T(8,128)(2,1)S(1)}, u32[]{:S(2)}, u32[]{:S(2)}) collective-permute-start(bf16[2,512,512]{2,1,0:T(8,128)(2,1)S(1)} %collective-permute-done.9), channel_id=1, source_target_pairs={{0,8},{12,4},{8,16},{20,12},{16,24},{28,20},{1,9},{13,5},{9,17},{2... | collective-permute-start | bytes 3145736 | tf_op jit(solution)/shard_map/ppermute | solution.py:505
  96.3 4.0 %copy-start = (f32[1024,2560]{1,0:T(8,128)S(1)}, f32[1024,2560]{1,0:T(8,128)}, u32[]{:S(2)}) copy-start(f32[1024,2560]{1,0:T(8,128)} %shard_map.130.part_ref) | copy-start | bytes 31457284
  100.2 18.6 %copy-start.4 = (s32[18]{0:T(128)S(1)}, s32[18]{0:T(128)}, u32[]{:S(2)}) copy-start(s32[18]{0:T(128)} %get-tuple-element.16.meta_ref) | copy-start | bytes 220

commit v4 on v3

--- a/solution.py
+++ b/solution.py
@@ -467,7 +467,7 @@
     if count <= 8:
         shards = [both] + [
             lax.ppermute(both, "seq", [(i, (i + 2 * k) % count) for i in range(count)])
-            for k in range(1, count // 2)
+            for k in range(count // 2 - 1, 0, -1)
         ]
     else:
         groups = [list(range(start, count, 2)) for start in range(2)]

time: 135 us -> 135 us (level); the launches traced: 135 us -> 134 us
  waiting for transfers between devices: 48.5 us -> 45.5 us
  starting transfers between devices: 18.3 us -> 19.9 us
    ppermute x2, waiting for transfers between devices: 6.09 us -> 4.21 us  [local(): arrived = lax.ppermute(after(parcel, *gate), 'seq', straight)]
    ppermute x2, starting transfers between devices: 4.34 us -> 5.91 us  [local(): arrived = lax.ppermute(after(parcel, *gate), 'seq', straight)]
  transfers between devices with their start and end apart: 11 -> 11, of which waited for: 7 -> 5; matrix products, arithmetic and copies ran while one was open for 9% -> 9% of each run, Pallas kernels for 30% -> 31%
where the time goes in v4:
time: 135 us; the launch traced here: 134 us
  Pallas kernels  49.4 us (37%)
  waiting for transfers between devices  45.5 us (34%)
  starting transfers between devices  19.9 us (15%)
  local copies, waits for them, and re-layouts  13.6 us (10%)
  other arithmetic  4.93 us (4%)
    ppermute x3, waiting for transfers between devices, local(): lax.ppermute(both, 'seq', [(i, (i + 2 * k) % count) for i in range(count)])  26 us
    pallas_call x3, Pallas kernels, attend_rest(): pl.pallas_call(functools.partial(rest_kernel, len(shards)), grid_spec=plt...  20.4 us
    pallas_call x1, Pallas kernels, attend_own(): pl.pallas_call(own_kernel, grid_spec=pltpu.PrefetchScalarGridSpec(num_sca...  18.5 us
    ppermute x1, waiting for transfers between devices, local(): forwarded = lax.ppermute(arrived, 'seq', relayed)  9.08 us
    pallas_call x1, Pallas kernels, turn(): pl.pallas_call(turn_kernel, grid_spec=pltpu.PrefetchScalarGridSpec(num_sc...  6.49 us
    unnamed x32, local copies, waits for them, and re-layouts  6.46 us
    ppermute x1, waiting for transfers between devices, local(): near_values = lax.ppermute(pair_values[None], 'seq', pair)  6.2 us
    ppermute x2, starting transfers between devices, local(): arrived = lax.ppermute(after(parcel, *gate), 'seq', straight)  5.91 us
  transfers between devices with their start and end apart: 11, of which 5 were waited for; matrix products, arithmetic and copies ran while one was open for 9% of the time, Pallas kernels for 31%

profile of v4, /device:TPU:8, one launch (start us, length us, event | category | flops | bytes accessed | tf_op | source)
XLA Modules:
  0.0 133.6 jit_solution(8004352243627623946)
XLA Ops:
  0.0 2.4 %shard_map.128 = bf16[2,2,32,1280]{3,2,1,0:T(8,128)(2,1)} custom-call(s32[2]{0:T(128)} %owner_ref.1, bf16[8,32,1280]{2,1,0:T(8,128)(2,1)} %keys_ref.1, bf16[8,32,1280]{2,1,0:T(8,128)(2,1)} %values_ref.1), custom_call_target="tpu_custom_call" | custom-call | flops 1000 | bytes 1000 | tf_op jit(solution)/shard_map/pallas_call | solution.py:215
  2.4 1.5 %collective-permute-start.3 = (bf16[2,2,32,1280]{3,2,1,0:T(8,128)(2,1)}, bf16[2,2,32,1280]{3,2,1,0:T(8,128)(2,1)}, u32[]{:S(2)}, u32[]{:S(2)}) collective-permute-start(bf16[2,2,32,1280]{3,2,1,0:T(8,128)(2,1)} %shard_map.128), channel_id=1, source_target_pairs={{0,4},{4,0},{8,12},{12,8},{16,20},{20,16},{24,28},{28,24},{1,5},{5... | collective-permute-start | bytes 983048 | tf_op jit(solution)/shard_map/ppermute | solution.py:464
  3.9 3.6 %multiply_reduce_fusion = (f32[1024]{0:T(1024)S(1)}, f32[1024]{0:T(1024)S(1)}) fusion(bf16[1024,1280]{1,0:T(8,128)(2,1)} %refs_1_.1, bf16[1024,1280]{1,0:T(8,128)(2,1)} %refs_0_.1), kind=kLoop, calls=%fused_computation | loop fusion | flops 7862272 | bytes 5251072 | tf_op jit(solution)/shard_map/reduce_sum | solution.py:481
  7.5 0.1 collective-permute-start
  7.6 0.0 copy-start.15
  7.6 0.0 copy-start.14
  7.6 0.0 copy-start.12
  7.7 0.0 copy-start.13
  7.7 0.0 copy-start.1
  7.7 0.0 copy-start.5
  7.7 0.0 copy-start.6
  7.7 2.6 %dynamic-slice_bitcast_fusion = bf16[1,512,1280]{2,1,0:T(8,128)(2,1)} fusion(bf16[1024,1280]{1,0:T(8,128)(2,1)} %v_ref.1, s32[]{:T(128)S(6)} %select_n.17), kind=kLoop, calls=%fused_computation.3 | loop fusion | bytes 2621444 | tf_op jit(solution)/shard_map/broadcast_in_dim | solution.py:466
  10.3 0.5 collective-permute-start.8
  10.8 1.2 dynamic-slice_bitcast_fusion.2
  12.0 0.0 collective-permute-done
  12.1 1.6 %collective-permute-start.1 = (f32[2,1024]{1,0:T(2,128)S(1)}, f32[2,1024]{1,0:T(2,128)S(1)}, u32[]{:S(2)}, u32[]{:S(2)}) collective-permute-start(f32[2,1024]{1,0:T(2,128)S(1)} %fusion), channel_id=1, source_target_pairs={{0,2},{1,3},{2,0},{3,1},{4,6},{5,7},{6,4},{7,5},{8,10},{9,11},{10,... | collective-permute-start | bytes 24584 | tf_op jit(solution)/shard_map/ppermute | solution.py:125
  13.7 1.9 %dynamic-slice_bitcast_fusion.4 = bf16[1,512,512]{2,1,0:T(8,128)(2,1)} fusion(bf16[1024,1280]{1,0:T(8,128)(2,1)} %v_ref.1, s32[]{:T(128)S(6)} %select_n.16), kind=kLoop, calls=%fused_computation.9 | loop fusion | bytes 1048580 | tf_op jit(solution)/shard_map/stack | solution.py:501
  15.5 0.6 reshape.16.shapes_ref
  16.1 0.7 reshape.17.windows_ref
  16.8 1.5 %shard_map.127 = (s32[24]{0:T(128)}, s32[64]{0:T(128)}, s32[18]{0:T(128)}, s32[18]{0:T(128)}) custom-call(s32[1]{0:T(128)} %bitcast.me_ref, s32[6]{0:T(128)} %reshape.16.shapes_ref, s32[216]{0:T(256)} %reshape.17.windows_ref), custom_call_target="tpu_custom_call" | custom-call | flops 1000 | bytes 1000 | tf_op jit(solution)/shard_map/pallas_call | solution.py:110
  18.4 0.0 copy-start.2
  18.4 1.7 %copy-done.2 = bf16[1024,1280]{1,0:T(8,128)(2,1)S(1)} copy-done((bf16[1024,1280]{1,0:T(8,128)(2,1)S(1)}, bf16[1024,1280]{1,0:T(8,128)(2,1)}, u32[]{:S(2)}) %copy-start.2) | copy-done | bytes 2621464
  20.1 0.7 copy-done.8
  20.8 6.5 %shard_map.129 = (bf16[1024,1280]{1,0:T(8,128)(2,1)S(1)}, bf16[1024,1280]{1,0:T(8,128)(2,1)S(1)}) custom-call(s32[24]{0:T(128)S(1)} %copy-done.8, s32[1,128]{1,0:T(1,128)S(1)} %copy-done.5, f32[1,128]{1,0:T(1,128)S(1)} %copy-done.6, f32[2,1024]{1,0:T(2,128)S(1)} %fusion.1.squares_ref, bf16[1024,1280]{1,0:T(8,128)(2,1)S(1)} %copy-done.2, ...), custom_call_target="tpu_custom_call" | custom-call | flops 1000 | bytes 1000 | tf_op jit(solution)/shard_map/pallas_call | solution.py:182
  27.3 0.1 dynamic-slice_bitcast_fusion.3
  27.4 0.1 dynamic-slice_bitcast_fusion.1
  27.6 0.0 copy-start.3
  27.6 1.6 %collective-permute-start.2 = (bf16[1,512,1280]{2,1,0:T(8,128)(2,1)S(1)}, bf16[1,512,1280]{2,1,0:T(8,128)(2,1)S(1)}, u32[]{:S(2)}, u32[]{:S(2)}) collective-permute-start(bf16[1,512,1280]{2,1,0:T(8,128)(2,1)S(1)} %dynamic-slice_bitcast_fusion.1), channel_id=1, source_target_pairs={{0,4},{4,0},{8,12},{12,8},{16,20},{20,16},{24,28},{28,24},{1,5},{5... | collective-permute-start | bytes 3932168 | tf_op jit(solution)/shard_map/ppermute | solution.py:485
  29.1 0.1 pad_maximum_fusion
  29.3 0.1 pad_maximum_fusion.1
  29.4 1.0 pad_maximum_fusion.2.rest_0_
  30.5 0.5 collective-permute-start.4
  31.0 2.6 %collective-permute-start.5 = (bf16[2,2,64,1280]{3,2,1,0:T(8,128)(2,1)S(1)}, bf16[2,2,64,1280]{3,2,1,0:T(8,128)(2,1)S(1)}, u32[]{:S(2)}, u32[]{:S(2)}) collective-permute-start(bf16[2,2,64,1280]{3,2,1,0:T(8,128)(2,1)S(1)} %pad_maximum_fusion.2.rest_0_), channel_id=1, source_target_pairs={{0,16},{4,20},{8,24},{12,28},{16,0},{20,4},{24,8},{28,12},{1,17},{... | collective-permute-start | bytes 1966088 | tf_op jit(solution)/shard_map/ppermute | solution.py:469
  33.5 2.5 %collective-permute-start.6 = (bf16[2,2,64,1280]{3,2,1,0:T(8,128)(2,1)S(1)}, bf16[2,2,64,1280]{3,2,1,0:T(8,128)(2,1)S(1)}, u32[]{:S(2)}, u32[]{:S(2)}) collective-permute-start(bf16[2,2,64,1280]{3,2,1,0:T(8,128)(2,1)S(1)} %pad_maximum_fusion.2.rest_0_), channel_id=1, source_target_pairs={{0,8},{4,12},{8,16},{12,20},{16,24},{20,28},{24,0},{28,4},{1,9},{5... | collective-permute-start | bytes 1966088 | tf_op jit(solution)/shard_map/ppermute | solution.py:469
  36.0 6.2 %collective-permute-done.8.vn_ref = bf16[1,512,1280]{2,1,0:T(8,128)(2,1)} collective-permute-done((bf16[1,512,1280]{2,1,0:T(8,128)(2,1)}, bf16[1,512,1280]{2,1,0:T(8,128)(2,1)}, u32[]{:S(2)}, u32[]{:S(2)}) %collective-permute-start.8) | collective-permute-done | bytes 1310752 | tf_op jit(solution)/shard_map/ppermute | solution.py:466
  42.2 2.4 %collective-permute-start.9 = (bf16[2,512,512]{2,1,0:T(8,128)(2,1)S(1)}, bf16[2,512,512]{2,1,0:T(8,128)(2,1)S(1)}, u32[]{:S(2)}, u32[]{:S(2)}) collective-permute-start(bf16[2,512,512]{2,1,0:T(8,128)(2,1)S(1)} %pad_maximum_fusion.1), channel_id=1, source_target_pairs={{4,0},{8,12},{12,8},{16,20},{20,16},{24,28},{5,1},{9,13},{13,9},{1... | collective-permute-start | bytes 3145736 | tf_op jit(solution)/shard_map/ppermute | solution.py:503
  44.7 18.5 %shard_map.130.part_ref = f32[1024,2560]{1,0:T(8,128)} custom-call(s32[64]{0:T(128)S(1)} %copy-done.9, bf16[1024,1280]{1,0:T(8,128)(2,1)S(1)} %get-tuple-element.20.q_ref, bf16[1024,1280]{1,0:T(8,128)(2,1)S(1)} %get-tuple-element.22.k_ref, bf16[1024,1280]{1,0:T(8,128)(2,1)S(1)} %copy-done.3), custom_call_target="tpu_custom_call" | custom-call | flops 10737418240 | bytes 62914560 | tf_op jit(solution)/shard_map/pallas_call | solution.py:329
  63.2 13.0 %collective-permute-done.4.rest_1_ = bf16[2,2,64,1280]{3,2,1,0:T(8,128)(2,1)S(1)} collective-permute-done((bf16[2,2,64,1280]{3,2,1,0:T(8,128)(2,1)S(1)}, bf16[2,2,64,1280]{3,2,1,0:T(8,128)(2,1)S(1)}, u32[]{:S(2)}, u32[]{:S(2)}) %collective-permute-start.4) | collective-permute-done | bytes 655392 | tf_op jit(solution)/shard_map/ppermute | solution.py:469
  76.2 0.0 collective-permute-done.5.rest_2_
  76.3 12.9 %collective-permute-done.6.rest_3_ = bf16[2,2,64,1280]{3,2,1,0:T(8,128)(2,1)S(1)} collective-permute-done((bf16[2,2,64,1280]{3,2,1,0:T(8,128)(2,1)S(1)}, bf16[2,2,64,1280]{3,2,1,0:T(8,128)(2,1)S(1)}, u32[]{:S(2)}, u32[]{:S(2)}) %collective-permute-start.6) | collective-permute-done | bytes 655392 | tf_op jit(solution)/shard_map/ppermute | solution.py:469
  89.2 3.5 %collective-permute-start.7 = (bf16[2,512,768]{2,1,0:T(8,128)(2,1)S(1)}, bf16[2,512,768]{2,1,0:T(8,128)(2,1)S(1)}, u32[]{:S(2)}, u32[]{:S(2)}) collective-permute-start(bf16[2,512,768]{2,1,0:T(8,128)(2,1)S(1)} %pad_maximum_fusion), channel_id=1, source_target_pairs={{4,8},{8,4},{12,16},{16,12},{20,24},{24,20},{5,9},{9,5},{13,17},{1... | collective-permute-start | bytes 4718600 | tf_op jit(solution)/shard_map/ppermute | solution.py:503
  92.7 3.2 %collective-permute-start.10 = (bf16[2,512,512]{2,1,0:T(8,128)(2,1)S(1)}, bf16[2,512,512]{2,1,0:T(8,128)(2,1)S(1)}, u32[]{:S(2)}, u32[]{:S(2)}) collective-permute-start(bf16[2,512,512]{2,1,0:T(8,128)(2,1)S(1)} %collective-permute-done.9), channel_id=1, source_target_pairs={{0,8},{12,4},{8,16},{20,12},{16,24},{28,20},{1,9},{13,5},{9,17},{2... | collective-permute-start | bytes 3145736 | tf_op jit(solution)/shard_map/ppermute | solution.py:505
  95.9 4.0 %copy-done = f32[1024,2560]{1,0:T(8,128)S(1)} copy-done((f32[1024,2560]{1,0:T(8,128)S(1)}, f32[1024,2560]{1,0:T(8,128)}, u32[]{:S(2)}) %copy-start) | copy-done | bytes 10485784
  99.9 9.9 %shard_map.131.rest_4_ = bf16[1024,1280]{1,0:T(8,128)(2,1)} custom-call(s32[18]{0:T(128)S(1)} %copy-done.7, bf16[1024,1280]{1,0:T(8,128)(2,1)S(1)} %get-tuple-element.20.q_ref, f32[1024,2560]{1,0:T(8,128)S(1)} %copy-done, bf16[1,512,1280]{2,1,0:T(8,128)(2,1)S(1)} %collective-permute-done.2.kn_ref, bf16[1,512,1280]{2,1,0:T(8,128)(2,1)} %collective-permute-done.8.vn_ref, ...), custom_call_target="tpu_custom_call" | custom-call | flops 4026531840 | bytes 23592960 | tf_op jit(solution)/shard_map/pallas_call | solution.py:412
  109.7 9.1 %collective-permute-done.10.kn_ref.vn_ref = bf16[2,512,512]{2,1,0:T(8,128)(2,1)S(1)} collective-permute-done((bf16[2,512,512]{2,1,0:T(8,128)(2,1)S(1)}, bf16[2,512,512]{2,1,0:T(8,128)(2,1)S(1)}, u32[]{:S(2)}, u32[]{:S(2)}) %collective-permute-start.10) | collective-permute-done | bytes 1048608 | tf_op jit(solution)/shard_map/ppermute | solution.py:505
  118.8 4.5 %shard_map.132.rest_4_ = bf16[1024,1280]{1,0:T(8,128)(2,1)} custom-call(s32[18]{0:T(128)S(1)} %copy-done.4, bf16[1024,1280]{1,0:T(8,128)(2,1)S(1)} %get-tuple-element.20.q_ref, f32[1024,2560]{1,0:T(8,128)S(1)} %copy-done, bf16[2,512,512]{2,1,0:T(8,128)(2,1)S(1)} %collective-permute-done.10.kn_ref.vn_ref, ...), custom_call_target="tpu_custom_call", output_to_operand_aliasing={{}: (9, {})} | custom-call | flops 1610612736 | bytes 9437184 | tf_op jit(solution)/shard_map/pallas_call | solution.py:412
  123.3 4.2 %collective-permute-done.7.kn_ref.vn_ref = bf16[2,512,768]{2,1,0:T(8,128)(2,1)S(1)} collective-permute-done((bf16[2,512,768]{2,1,0:T(8,128)(2,1)S(1)}, bf16[2,512,768]{2,1,0:T(8,128)(2,1)S(1)}, u32[]{:S(2)}, u32[]{:S(2)}) %collective-permute-start.7) | collective-permute-done | bytes 1572896 | tf_op jit(solution)/shard_map/ppermute | solution.py:503
  127.5 6.1 %shard_map.133 = bf16[1024,1280]{1,0:T(8,128)(2,1)} custom-call(s32[18]{0:T(128)S(1)} %copy-done.4, bf16[1024,1280]{1,0:T(8,128)(2,1)S(1)} %get-tuple-element.20.q_ref, f32[1024,2560]{1,0:T(8,128)S(1)} %copy-done, bf16[2,512,768]{2,1,0:T(8,128)(2,1)S(1)} %collective-permute-done.7.kn_ref.vn_ref, ...), custom_call_target="tpu_custom_call", output_to_operand_aliasing={{}: (9, {})} | custom-call | flops 2415919104 | bytes 14155776 | tf_op jit(solution)/shard_map/pallas_call | solution.py:412
  (30 shorter events, 0.1 us)
Async XLA Ops:
  2.4 27.0 %collective-permute-start.3 = (bf16[2,2,32,1280]{3,2,1,0:T(8,128)(2,1)}, bf16[2,2,32,1280]{3,2,1,0:T(8,128)(2,1)}, u32[]{:S(2)}, u32[]{:S(2)}) collective-permute-start(bf16[2,2,32,1280]{3,2,1,0:T(8,128)(2,1)} %shard_map.128), channel_id=1, source_target_pairs={{0,4},{4,0},{8,12},{12,8},{16,20},{20,16},{24,28},{28,24},{1,5},{5... | collective-permute-start | bytes 983048 | tf_op jit(solution)/shard_map/ppermute | solution.py:464
  7.5 4.5 %collective-permute-start = (f32[2,1024]{1,0:T(2,128)S(1)}, f32[2,1024]{1,0:T(2,128)S(1)}, u32[]{:S(2)}, u32[]{:S(2)}) collective-permute-start(f32[2,1024]{1,0:T(2,128)S(1)} %pad_maximum_fusion.3), channel_id=1, source_target_pairs={{0,1},{1,0},{2,3},{3,2},{4,5},{5,4},{6,7},{7,6},{8,9},{9,8},{10,11... | collective-permute-start | bytes 24584 | tf_op jit(solution)/shard_map/ppermute | solution.py:125
  7.6 7.9 %copy-start.15 = (s32[2,3]{1,0:T(2,128)S(1)}, s32[2,3]{1,0:T(2,128)}, u32[]{:S(2)}) copy-start(s32[2,3]{1,0:T(2,128)} %param.18) | copy-start | bytes 76
  7.6 8.5 %copy-start.14 = (s32[8,27]{1,0:T(8,128)S(1)}, s32[8,27]{1,0:T(8,128)}, u32[]{:S(2)}) copy-start(s32[8,27]{1,0:T(8,128)} %param.19) | copy-start | bytes 2596
  7.6 10.6 %copy-start.12 = (f32[1280]{0:T(1024)S(1)}, f32[1280]{0:T(1024)}, u32[]{:S(2)}) copy-start(f32[1280]{0:T(1024)} %param.16) | copy-start | bytes 15364
  7.7 10.7 %copy-start.13 = (f32[1280]{0:T(1024)S(1)}, f32[1280]{0:T(1024)}, u32[]{:S(2)}) copy-start(f32[1280]{0:T(1024)} %param.17) | copy-start | bytes 15364
  7.7 10.7 %copy-start.1 = (bf16[1024,1280]{1,0:T(8,128)(2,1)S(1)}, bf16[1024,1280]{1,0:T(8,128)(2,1)}, u32[]{:S(2)}) copy-start(bf16[1024,1280]{1,0:T(8,128)(2,1)} %refs_1_.1) | copy-start | bytes 7864324
  7.7 10.7 %copy-start.5 = (s32[1,128]{1,0:T(1,128)S(1)}, s32[1,128]{1,0:T(1,128)}, u32[]{:S(2)}) copy-start(s32[1,128]{1,0:T(1,128)} %constant.39.part_ref) | copy-start | bytes 1540
  7.7 10.7 %copy-start.6 = (f32[1,128]{1,0:T(1,128)S(1)}, f32[1,128]{1,0:T(1,128)}, u32[]{:S(2)}) copy-start(f32[1,128]{1,0:T(1,128)} %constant.43.frequency_ref) | copy-start | bytes 1540
  10.3 31.9 %collective-permute-start.8 = (bf16[1,512,1280]{2,1,0:T(8,128)(2,1)}, bf16[1,512,1280]{2,1,0:T(8,128)(2,1)}, u32[]{:S(2)}, u32[]{:S(2)}) collective-permute-start(bf16[1,512,1280]{2,1,0:T(8,128)(2,1)} %dynamic-slice_bitcast_fusion), channel_id=1, source_target_pairs={{0,4},{4,0},{8,12},{12,8},{16,20},{20,16},{24,28},{28,24},{1,5},{5... | collective-permute-start | bytes 3932168 | tf_op jit(solution)/shard_map/ppermute | solution.py:466
  12.1 6.3 %collective-permute-start.1 = (f32[2,1024]{1,0:T(2,128)S(1)}, f32[2,1024]{1,0:T(2,128)S(1)}, u32[]{:S(2)}, u32[]{:S(2)}) collective-permute-start(f32[2,1024]{1,0:T(2,128)S(1)} %fusion), channel_id=1, source_target_pairs={{0,2},{1,3},{2,0},{3,1},{4,6},{5,7},{6,4},{7,5},{8,10},{9,11},{10,... | collective-permute-start | bytes 24584 | tf_op jit(solution)/shard_map/ppermute | solution.py:125
  18.4 1.7 %copy-start.2 = (bf16[1024,1280]{1,0:T(8,128)(2,1)S(1)}, bf16[1024,1280]{1,0:T(8,128)(2,1)}, u32[]{:S(2)}) copy-start(bf16[1024,1280]{1,0:T(8,128)(2,1)} %refs_0_.1) | copy-start | bytes 7864324
  20.1 0.7 copy-start.8
  27.5 1.8 %copy-start.10 = (bf16[1,512,512]{2,1,0:T(8,128)(2,1)S(1)}, bf16[1,512,512]{2,1,0:T(8,128)(2,1)}, u32[]{:S(2)}) copy-start(bf16[1,512,512]{2,1,0:T(8,128)(2,1)} %dynamic-slice_bitcast_fusion.4) | copy-start | bytes 1572868
  27.6 1.9 %copy-start.11 = (bf16[2,2,32,1280]{3,2,1,0:T(8,128)(2,1)S(1)}, bf16[2,2,32,1280]{3,2,1,0:T(8,128)(2,1)}, u32[]{:S(2)}) copy-start(bf16[2,2,32,1280]{3,2,1,0:T(8,128)(2,1)} %shard_map.128) | copy-start | bytes 983044
  27.6 17.1 %copy-start.3 = (bf16[1024,1280]{1,0:T(8,128)(2,1)S(1)}, bf16[1024,1280]{1,0:T(8,128)(2,1)}, u32[]{:S(2)}) copy-start(bf16[1024,1280]{1,0:T(8,128)(2,1)} %v_ref.1) | copy-start | bytes 7864324
  27.6 17.1 %copy-start.9 = (s32[64]{0:T(128)S(1)}, s32[64]{0:T(128)}, u32[]{:S(2)}) copy-start(s32[64]{0:T(128)} %get-tuple-element.21.meta_ref) | copy-start | bytes 772
  27.6 61.6 %collective-permute-start.2 = (bf16[1,512,1280]{2,1,0:T(8,128)(2,1)S(1)}, bf16[1,512,1280]{2,1,0:T(8,128)(2,1)S(1)}, u32[]{:S(2)}, u32[]{:S(2)}) collective-permute-start(bf16[1,512,1280]{2,1,0:T(8,128)(2,1)S(1)} %dynamic-slice_bitcast_fusion.1), channel_id=1, source_target_pairs={{0,4},{4,0},{8,12},{12,8},{16,20},{20,16},{24,28},{28,24},{1,5},{5... | collective-permute-start | bytes 3932168 | tf_op jit(solution)/shard_map/ppermute | solution.py:485
  30.5 45.8 %collective-permute-start.4 = (bf16[2,2,64,1280]{3,2,1,0:T(8,128)(2,1)S(1)}, bf16[2,2,64,1280]{3,2,1,0:T(8,128)(2,1)S(1)}, u32[]{:S(2)}, u32[]{:S(2)}) collective-permute-start(bf16[2,2,64,1280]{3,2,1,0:T(8,128)(2,1)S(1)} %pad_maximum_fusion.2.rest_0_), channel_id=1, source_target_pairs={{0,24},{4,28},{8,0},{12,4},{16,8},{20,12},{24,16},{28,20},{1,25},{... | collective-permute-start | bytes 1966088 | tf_op jit(solution)/shard_map/ppermute | solution.py:469
  31.0 45.3 %collective-permute-start.5 = (bf16[2,2,64,1280]{3,2,1,0:T(8,128)(2,1)S(1)}, bf16[2,2,64,1280]{3,2,1,0:T(8,128)(2,1)S(1)}, u32[]{:S(2)}, u32[]{:S(2)}) collective-permute-start(bf16[2,2,64,1280]{3,2,1,0:T(8,128)(2,1)S(1)} %pad_maximum_fusion.2.rest_0_), channel_id=1, source_target_pairs={{0,16},{4,20},{8,24},{12,28},{16,0},{20,4},{24,8},{28,12},{1,17},{... | collective-permute-start | bytes 1966088 | tf_op jit(solution)/shard_map/ppermute | solution.py:469
  33.5 55.7 %collective-permute-start.6 = (bf16[2,2,64,1280]{3,2,1,0:T(8,128)(2,1)S(1)}, bf16[2,2,64,1280]{3,2,1,0:T(8,128)(2,1)S(1)}, u32[]{:S(2)}, u32[]{:S(2)}) collective-permute-start(bf16[2,2,64,1280]{3,2,1,0:T(8,128)(2,1)S(1)} %pad_maximum_fusion.2.rest_0_), channel_id=1, source_target_pairs={{0,8},{4,12},{8,16},{12,20},{16,24},{20,28},{24,0},{28,4},{1,9},{5... | collective-permute-start | bytes 1966088 | tf_op jit(solution)/shard_map/ppermute | solution.py:469
  42.2 50.5 %collective-permute-start.9 = (bf16[2,512,512]{2,1,0:T(8,128)(2,1)S(1)}, bf16[2,512,512]{2,1,0:T(8,128)(2,1)S(1)}, u32[]{:S(2)}, u32[]{:S(2)}) collective-permute-start(bf16[2,512,512]{2,1,0:T(8,128)(2,1)S(1)} %pad_maximum_fusion.1), channel_id=1, source_target_pairs={{4,0},{8,12},{12,8},{16,20},{20,16},{24,28},{5,1},{9,13},{13,9},{1... | collective-permute-start | bytes 3145736 | tf_op jit(solution)/shard_map/ppermute | solution.py:503
  44.7 51.2 %copy-start.7 = (s32[18]{0:T(128)S(1)}, s32[18]{0:T(128)}, u32[]{:S(2)}) copy-start(s32[18]{0:T(128)} %get-tuple-element.26.meta_ref) | copy-start | bytes 220
  89.2 38.3 %collective-permute-start.7 = (bf16[2,512,768]{2,1,0:T(8,128)(2,1)S(1)}, bf16[2,512,768]{2,1,0:T(8,128)(2,1)S(1)}, u32[]{:S(2)}, u32[]{:S(2)}) collective-permute-start(bf16[2,512,768]{2,1,0:T(8,128)(2,1)S(1)} %pad_maximum_fusion), channel_id=1, source_target_pairs={{4,8},{8,4},{12,16},{16,12},{20,24},{24,20},{5,9},{9,5},{13,17},{1... | collective-permute-start | bytes 4718600 | tf_op jit(solution)/shard_map/ppermute | solution.py:503
  92.7 26.1 %collective-permute-start.10 = (bf16[2,512,512]{2,1,0:T(8,128)(2,1)S(1)}, bf16[2,512,512]{2,1,0:T(8,128)(2,1)S(1)}, u32[]{:S(2)}, u32[]{:S(2)}) collective-permute-start(bf16[2,512,512]{2,1,0:T(8,128)(2,1)S(1)} %collective-permute-done.9), channel_id=1, source_target_pairs={{0,8},{12,4},{8,16},{20,12},{16,24},{28,20},{1,9},{13,5},{9,17},{2... | collective-permute-start | bytes 3145736 | tf_op jit(solution)/shard_map/ppermute | solution.py:505
  95.9 4.0 %copy-start = (f32[1024,2560]{1,0:T(8,128)S(1)}, f32[1024,2560]{1,0:T(8,128)}, u32[]{:S(2)}) copy-start(f32[1024,2560]{1,0:T(8,128)} %shard_map.130.part_ref) | copy-start | bytes 31457284
  99.9 18.9 %copy-start.4 = (s32[18]{0:T(128)S(1)}, s32[18]{0:T(128)}, u32[]{:S(2)}) copy-start(s32[18]{0:T(128)} %get-tuple-element.16.meta_ref) | copy-start | bytes 220
